TPU v7x, 32 devices: a whole 2x2x4 slice. The times are simulated.
32 devices in a mesh: scene: 8 (over y, x, core), kd: 4 (over z).
Axes of the slice: x: 2, y: 2, z: 4, core: 2. Of those that a mesh axis runs over, the one named last changes fastest.
Arguments:
- features: bfloat16 [8, 16, 512, 128], P('scene', 'kd'), may hold values from -6 to 6
- send_faces: int32 [8, 4, 2, 1], P('scene', 'kd'), may hold values from 0 to 23, as said below
- face_source: int32 [8, 16, 6], P('scene', 'kd'), may hold values from 0 to 26, as said below
- cotangent: bfloat16 [8, 16, 64, 256], P('scene', 'kd'), may hold values from -8 to 8
- conv_one: bfloat16 [7, 128, 128], replicated, may hold values from -0.1875 to 0.1875
- down_weight: bfloat16 [1024, 256], replicated, may hold values from -0.1875 to 0.1875
- conv_two: bfloat16 [7, 256, 256], replicated, may hold values from -0.125 to 0.125
Outputs:
- encoded: bfloat16 [8, 16, 64, 256], P('scene', 'kd')
- grad_conv_one: float32 [7, 128, 128], replicated
- grad_down: float32 [1024, 256], replicated
- grad_conv_two: float32 [7, 256, 256], replicated
Inputs may be any that keep to these rules, and one draw needn't show every extreme that they name: `send_faces`: entry [i, t] names face 6 b + s of the sender's own brick b; across bit i every device sends exactly one face, of side 2 (i mod 3) + 1 where its bit i is 0 and of side 2 (i mod 3) where it is 1; no face is named twice on a device. `face_source`: for brick b and direction s: a value under 6 * 4 is a local face, of the side opposite s; 24 + i + t is slot t received across bit i; 26 is no neighbour. The relation is symmetric: where direction s of brick b takes a face of brick b2, direction opposite s of b2 takes the face of b at side s, across devices through the same bit and slot.
All inputs are finite; a program needn't handle non-finite values.
Results may differ from a plain program's by a relative error of at most 0.0065.
Values may be sent and summed in bfloat16 or wider, within the bound.
A program may use at most 64 MiB of HBM per device.

v0:
```python
import jax
import jax.numpy as jnp
from jax import lax
from jax.sharding import PartitionSpec as P

OPPOSITE = (0, 2, 1, 4, 3, 6, 5)


def swapped(value, axis, stride):
    mask = 2**stride
    pairs = [(source, source ^ mask) for source in range(lax.axis_size(axis))]
    return lax.ppermute(value, axis, pairs)


def face_slabs(blocks):
    return jnp.stack(
        [
            blocks[:, 0],
            blocks[:, -1],
            blocks[:, :, 0],
            blocks[:, :, -1],
            blocks[:, :, :, 0],
            blocks[:, :, :, -1],
        ],
        axis=1,
    )


def shift_taps(blocks, border):
    return [
        blocks,
        jnp.concatenate([border[:, 0][:, None], blocks[:, :-1]], 1),
        jnp.concatenate([blocks[:, 1:], border[:, 1][:, None]], 1),
        jnp.concatenate([border[:, 2][:, :, None], blocks[:, :, :-1]], 2),
        jnp.concatenate([blocks[:, :, 1:], border[:, 3][:, :, None]], 2),
        jnp.concatenate([border[:, 4][:, :, :, None], blocks[:, :, :, :-1]], 3),
        jnp.concatenate([blocks[:, :, :, 1:], border[:, 5][:, :, :, None]], 3),
    ]


def conv_apply(taps, weight):
    chans = taps[0].shape[-1]
    total = jnp.dot(taps[0].reshape(-1, chans), weight[0], preferred_element_type=jnp.float32)
    for tap_index in range(1, 7):
        total = total + jnp.dot(
            taps[tap_index].reshape(-1, chans),
            weight[tap_index],
            preferred_element_type=jnp.float32,
        )
    return total


def conv_back(taps, weight):
    chans = taps[0].shape[-1]
    total = lax.dot_general(
        taps[0].reshape(-1, chans),
        weight[0],
        (((1,), (1,)), ((), ())),
        preferred_element_type=jnp.float32,
    )
    for tap_index in range(1, 7):
        total = total + lax.dot_general(
            taps[OPPOSITE[tap_index]].reshape(-1, chans),
            weight[tap_index],
            (((1,), (1,)), ((), ())),
            preferred_element_type=jnp.float32,
        )
    return total


def weight_grads(taps, delta):
    chans = taps[0].shape[-1]
    return jnp.stack(
        [
            lax.dot_general(
                single.reshape(-1, chans),
                delta,
                (((0,), (0,)), ((), ())),
                preferred_element_type=jnp.float32,
            )
            for single in taps
        ]
    )


def down_rows(hidden, brick_count, chans):
    return (
        hidden.reshape(brick_count, 4, 2, 4, 2, 4, 2, chans)
        .transpose(0, 1, 3, 5, 2, 4, 6, 7)
        .reshape(brick_count * 64, 8 * chans)
    )


def up_rows(patch_grad, brick_count, chans):
    return (
        patch_grad.reshape(brick_count, 4, 4, 4, 2, 2, 2, chans)
        .transpose(0, 1, 4, 2, 5, 3, 6, 7)
        .reshape(brick_count * 512, chans)
    )


def silu_slope(value):
    sigma = jax.nn.sigmoid(value)
    return sigma * (1.0 + value * (1.0 - sigma))


def rims_local(blocks, send_list, source_list, swapper):
    brick_count = blocks.shape[0]
    side_cells = blocks.shape[1]
    chans = blocks.shape[-1]
    faces = face_slabs(blocks).reshape(brick_count * 6, side_cells, side_cells, chans)
    pieces = [faces]
    for bit_index in range(send_list.shape[0]):
        pieces.append(swapper(faces[send_list[bit_index]], bit_index))
    pieces.append(jnp.zeros((1, side_cells, side_cells, chans), faces.dtype))
    lookup = jnp.concatenate(pieces, axis=0)
    return lookup[source_list.reshape(-1)].reshape(brick_count, 6, side_cells, side_cells, chans)


def on_device(features, send_faces, face_source, cotangent, conv_one, down_weight, conv_two):
    send_list = send_faces[0, 0]
    source_list = face_source[0]
    brick_count = features.shape[1]
    chan_one = features.shape[3]
    chan_two = cotangent.shape[3]
    grid_one = features[0].reshape(brick_count, 8, 8, 8, chan_one)
    border_one = rims_local(
        grid_one, send_list, source_list, lambda buffer, bit_index: swapped(buffer, "kd", bit_index)
    )
    taps_one = shift_taps(grid_one, border_one)
    pre_one = conv_apply(taps_one, conv_one)
    hidden_one = (
        features[0].reshape(-1, chan_one).astype(jnp.float32) + jax.nn.silu(pre_one)
    ).astype(jnp.bfloat16)
    patches = down_rows(hidden_one, brick_count, chan_one)
    coarse = jnp.dot(patches, down_weight, preferred_element_type=jnp.float32).astype(jnp.bfloat16)
    grid_two = coarse.reshape(brick_count, 4, 4, 4, chan_two)
    border_two = rims_local(
        grid_two, send_list, source_list, lambda buffer, bit_index: swapped(buffer, "kd", bit_index)
    )
    taps_two = shift_taps(grid_two, border_two)
    pre_two = conv_apply(taps_two, conv_two)
    encoded = (coarse.astype(jnp.float32) + jax.nn.silu(pre_two)).astype(jnp.bfloat16)
    upstream = cotangent[0].reshape(-1, chan_two).astype(jnp.float32)
    delta_two = (upstream * silu_slope(pre_two)).astype(jnp.bfloat16)
    grid_delta = delta_two.reshape(brick_count, 4, 4, 4, chan_two)
    border_delta = rims_local(
        grid_delta,
        send_list,
        source_list,
        lambda buffer, bit_index: swapped(buffer, "kd", bit_index),
    )
    taps_delta = shift_taps(grid_delta, border_delta)
    grad_two = weight_grads(taps_two, delta_two)
    grad_coarse = (upstream + conv_back(taps_delta, conv_two)).astype(jnp.bfloat16)
    grad_down = lax.dot_general(
        patches, grad_coarse, (((0,), (0,)), ((), ())), preferred_element_type=jnp.float32
    )
    patch_grad = lax.dot_general(
        grad_coarse, down_weight, (((1,), (1,)), ((), ())), preferred_element_type=jnp.float32
    )
    delta_one = (up_rows(patch_grad, brick_count, chan_one) * silu_slope(pre_one)).astype(
        jnp.bfloat16
    )
    grad_one = weight_grads(taps_one, delta_one)
    grad_one, grad_down, grad_two = lax.psum((grad_one, grad_down, grad_two), ("scene", "kd"))
    return (encoded.reshape(1, brick_count, 64, chan_two), grad_one, grad_down, grad_two)


def solution(mesh):
    placed = (
        P("scene", "kd", None, None),
        P("scene", "kd", None, None),
        P("scene", "kd", None),
        P("scene", "kd", None, None),
        P(),
        P(),
        P(),
    )
    return jax.shard_map(
        on_device,
        mesh=mesh,
        in_specs=placed,
        out_specs=(P("scene", "kd", None, None), P(), P(), P()),
        check_vma=False,
    )
```

profile of v0, /device:TPU:0, one launch (start us, length us, event | category | flops | bytes accessed | tf_op | source)
XLA Modules:
  0.0 266.5 jit_solution(12839304574601870475)
XLA Ops:
  7.2 0.9 slice_dynamic-update-slice_fusion.1
  8.2 1.4 fusion.68
  9.6 1.3 fusion.77
  13.5 0.9 slice_dynamic-update-slice_fusion
  14.4 0.9 fusion.48
  15.2 0.9 fusion.47
  17.4 4.1 %collective-permute-start.1 = (bf16[1,8,8,128]{3,2,1,0:T(8,128)(2,1)S(1)}, bf16[1,8,8,128]{3,2,1,0:T(8,128)(2,1)S(1)}, u32[]{:S(2)}, u32[]{:S(2)}) collective-permute-start(bf16[1,8,8,128]{3,2,1,0:T(8,128)(2,1)S(1)} %get-tuple-element.104), channel_id=1, source_target_pairs={{0,2},{1,3},{2,0},{3,1},{4,6},{5,7},{6,4},{7,5},{8,10},{9,11},{10,... | collective-permute-start | bytes 49160 | tf_op jit(solution)/shard_map/ppermute | solution.py:12
  21.5 1.6 collective-permute-start
  23.1 1.2 fusion.67
  24.3 1.1 fusion.66
  25.4 1.2 fusion.65
  28.0 1.3 pad_maximum_fusion
  33.1 1.4 add_convert_fusion
  34.6 1.2 copy.202
  35.8 1.4 reshape.156
  38.4 0.8 fusion.73
  39.2 1.8 fusion.31
  42.9 3.0 %collective-permute-done.3 = bf16[1,4,4,256]{3,2,1,0:T(4,128)(2,1)S(1)} collective-permute-done((bf16[1,4,4,256]{3,2,1,0:T(4,128)(2,1)S(1)}, bf16[1,4,4,256]{3,2,1,0:T(4,128)(2,1)S(1)}, u32[]{:S(2)}, u32[]{:S(2)}) %collective-permute-start.3) | collective-permute-done | bytes 8224 | tf_op jit(solution)/shard_map/ppermute | solution.py:12
  46.0 1.4 gather_fusion.1
  47.4 1.6 slice_bitcast_fusion.14
  49.0 1.0 pad_maximum_fusion.6
  50.0 1.7 pad_maximum_fusion.7
  51.7 0.9 reshape.161
  52.7 1.7 pad_maximum_fusion.8
  54.4 1.6 reshape.162
  56.0 1.7 pad_maximum_fusion.9
  57.6 1.6 reshape.163
  59.2 0.8 copy.146
  60.1 1.7 pad_maximum_fusion.10
  61.8 1.6 reshape.164
  63.3 0.8 copy.147
  64.2 1.7 pad_maximum_fusion.11
  65.9 1.6 reshape.165
  67.5 1.3 convolution_add_fusion.17
  68.8 1.1 convolution_add_fusion.16
  69.9 1.2 convolution_add_fusion.15
  71.5 1.0 fusion.16
  72.5 0.9 fusion.29
  75.6 2.1 collective-permute-start.5
  79.6 0.8 fusion.70
  81.5 1.4 gather_fusion.2
  83.0 1.5 slice_bitcast_fusion.6
  84.5 1.0 pad_maximum_fusion.12
  86.2 1.0 pad_maximum_fusion.13
  87.9 1.0 pad_maximum_fusion.14
  89.6 1.0 pad_maximum_fusion.15
  91.3 0.8 copy.157
  92.1 1.0 pad_maximum_fusion.16
  93.8 0.8 copy.158
  94.6 1.0 pad_maximum_fusion.17
  96.4 1.2 convolution_add_fusion.11
  97.6 1.2 convolution_add_fusion.10
  98.8 1.2 convolution_add_fusion.9
  100.0 1.1 convolution_add_fusion.8
  101.2 1.1 convolution_add_fusion.7
  102.3 1.1 fusion.8
  103.5 1.3 fusion.78
  104.8 1.5 fusion.79
  106.3 3.1 %reshape.176 = f32[4,4,4,4,2,2,2,128]{7,6,5,4,3,2,1,0:T(2,128)} reshape(f32[256,1024]{1,0:T(8,128)} %fusion.78) | data formatting | bytes 2097152 | tf_op jit(solution)/shard_map/reshape | solution.py:96
  109.4 1.8 copy.159
  115.0 139.1 %all-reduce.3.cloned.1.call-done = (f32[7,128,128]{1,2,0:T(8,128)}, f32[1024,256]{1,0:T(8,128)}, f32[7,256,256]{2,1,0:T(8,128)}) async-done(((f32[7,128,128]{1,2,0:T(8,128)}, f32[1024,256]{1,0:T(8,128)}, f32[7,256,256]{2,1,0:T(8,128)}), (f32[7,128,128]{1,2,0:T(8,128)}, f32[1024,256]{1,0:T(8,128)}, f32[7,256,256]{2,1,0:T(8,128)})) %all-reduce.3.cloned.1.call-update) | async-done | bytes 3342352 | tf_op jit(solution)/shard_map/psum | solution.py:166
  254.0 2.0 copy.166
  256.0 2.4 copy.233
  258.4 1.2 copy.234
  (153 shorter events, 21.8 us)
Async XLA Ops:
  7.2 30.0 %copy-start = (bf16[1024,256]{1,0:T(8,128)(2,1)S(1)}, bf16[1024,256]{1,0:T(8,128)(2,1)}, u32[]{:S(2)}) copy-start(bf16[1024,256]{1,0:T(8,128)(2,1)} %param.12) | copy-start | bytes 1572868
  7.2 15.9 %copy-start.1 = (bf16[1,4,512,128]{3,2,1,0:T(8,128)(2,1)S(1)}, bf16[1,4,512,128]{3,2,1,0:T(8,128)(2,1)}, u32[]{:S(2)}) copy-start(bf16[1,4,512,128]{3,2,1,0:T(8,128)(2,1)} %param.7) | copy-start | bytes 1572868
  7.2 246.8 %all-reduce.3.cloned.1.call-start = ((), (), s32[]{:S(2)}) async-start(), calls=%async_computation | async-start | bytes 6684672 | tf_op jit(solution)/shard_map/psum | solution.py:166
  17.4 9.5 %collective-permute-start.1 = (bf16[1,8,8,128]{3,2,1,0:T(8,128)(2,1)S(1)}, bf16[1,8,8,128]{3,2,1,0:T(8,128)(2,1)S(1)}, u32[]{:S(2)}, u32[]{:S(2)}) collective-permute-start(bf16[1,8,8,128]{3,2,1,0:T(8,128)(2,1)S(1)} %get-tuple-element.104), channel_id=1, source_target_pairs={{0,2},{1,3},{2,0},{3,1},{4,6},{5,7},{6,4},{7,5},{8,10},{9,11},{10,... | collective-permute-start | bytes 49160 | tf_op jit(solution)/shard_map/ppermute | solution.py:12
  21.5 5.4 %collective-permute-start = (bf16[1,8,8,128]{3,2,1,0:T(8,128)(2,1)S(1)}, bf16[1,8,8,128]{3,2,1,0:T(8,128)(2,1)S(1)}, u32[]{:S(2)}, u32[]{:S(2)}) collective-permute-start(bf16[1,8,8,128]{3,2,1,0:T(8,128)(2,1)S(1)} %get-tuple-element.103), channel_id=1, source_target_pairs={{0,1},{1,0},{2,3},{3,2},{4,5},{5,4},{6,7},{7,6},{8,9},{9,8},{10,11... | collective-permute-start | bytes 49160 | tf_op jit(solution)/shard_map/ppermute | solution.py:12
  24.3 2.2 copy-start.35
  24.3 2.3 copy-start.32
  29.5 1.0 copy-start.13
  29.5 1.1 copy-start.14
  30.8 0.8 copy-start.2
  31.1 1.0 copy-start.10
  31.1 1.2 copy-start.11
  32.8 1.8 copy-start.4
  32.8 1.7 copy-start.8
  41.2 4.6 %collective-permute-start.3 = (bf16[1,4,4,256]{3,2,1,0:T(4,128)(2,1)S(1)}, bf16[1,4,4,256]{3,2,1,0:T(4,128)(2,1)S(1)}, u32[]{:S(2)}, u32[]{:S(2)}) collective-permute-start(bf16[1,4,4,256]{3,2,1,0:T(4,128)(2,1)S(1)} %get-tuple-element.122), channel_id=1, source_target_pairs={{0,2},{1,3},{2,0},{3,1},{4,6},{5,7},{6,4},{7,5},{8,10},{9,11},{10,... | collective-permute-start | bytes 24584 | tf_op jit(solution)/shard_map/ppermute | solution.py:12
  41.6 4.2 %collective-permute-start.2 = (bf16[1,4,4,256]{3,2,1,0:T(4,128)(2,1)S(1)}, bf16[1,4,4,256]{3,2,1,0:T(4,128)(2,1)S(1)}, u32[]{:S(2)}, u32[]{:S(2)}) collective-permute-start(bf16[1,4,4,256]{3,2,1,0:T(4,128)(2,1)S(1)} %get-tuple-element.121), channel_id=1, source_target_pairs={{0,1},{1,0},{2,3},{3,2},{4,5},{5,4},{6,7},{7,6},{8,9},{9,8},{10,11... | collective-permute-start | bytes 24584 | tf_op jit(solution)/shard_map/ppermute | solution.py:12
  50.0 18.8 %copy-start.15 = (bf16[256,256]{1,0:T(8,128)(2,1)}, bf16[256,256]{1,0:T(8,128)(2,1)S(1)}, u32[]{:S(2)}) copy-start(bf16[256,256]{1,0:T(8,128)(2,1)S(1)} %reshape.160) | copy-start | bytes 393220
  52.7 17.2 %copy-start.17 = (bf16[256,256]{1,0:T(8,128)(2,1)}, bf16[256,256]{1,0:T(8,128)(2,1)S(1)}, u32[]{:S(2)}) copy-start(bf16[256,256]{1,0:T(8,128)(2,1)S(1)} %reshape.161) | copy-start | bytes 393220
  67.4 3.6 %copy-start.6 = (bf16[7,256,256]{2,1,0:T(8,128)(2,1)S(1)}, bf16[7,256,256]{2,1,0:T(8,128)(2,1)}, u32[]{:S(2)}) copy-start(bf16[7,256,256]{2,1,0:T(8,128)(2,1)} %param.13) | copy-start | bytes 2752516
  67.5 3.6 %copy-start.20 = (bf16[256,256]{1,0:T(8,128)(2,1)S(1)}, bf16[256,256]{1,0:T(8,128)(2,1)}, u32[]{:S(2)}) copy-start(bf16[256,256]{1,0:T(8,128)(2,1)} %reshape.163) | copy-start | bytes 393220
  67.5 3.8 %copy-start.22 = (bf16[256,256]{1,0:T(8,128)(2,1)S(1)}, bf16[256,256]{1,0:T(8,128)(2,1)}, u32[]{:S(2)}) copy-start(bf16[256,256]{1,0:T(8,128)(2,1)} %reshape.164) | copy-start | bytes 393220
  67.5 4.0 %copy-start.27 = (bf16[256,256]{1,0:T(8,128)(2,1)S(1)}, bf16[256,256]{1,0:T(8,128)(2,1)}, u32[]{:S(2)}) copy-start(bf16[256,256]{1,0:T(8,128)(2,1)} %reshape.165) | copy-start | bytes 393220
  67.5 4.0 %copy-start.33 = (bf16[1,4,64,256]{3,2,1,0:T(8,128)(2,1)S(1)}, bf16[1,4,64,256]{3,2,1,0:T(8,128)(2,1)}, u32[]{:S(2)}) copy-start(bf16[1,4,64,256]{3,2,1,0:T(8,128)(2,1)} %param.10) | copy-start | bytes 393220
  73.4 4.7 %copy-start.16 = (bf16[256,256]{1,0:T(8,128)(2,1)S(1)}, bf16[256,256]{1,0:T(8,128)(2,1)}, u32[]{:S(2)}) copy-start(bf16[256,256]{1,0:T(8,128)(2,1)} %copy-done.15) | copy-start | bytes 393220
  73.4 4.9 %copy-start.18 = (bf16[256,256]{1,0:T(8,128)(2,1)S(1)}, bf16[256,256]{1,0:T(8,128)(2,1)}, u32[]{:S(2)}) copy-start(bf16[256,256]{1,0:T(8,128)(2,1)} %copy-done.17) | copy-start | bytes 393220
  73.5 5.2 %copy-start.19 = (bf16[256,256]{1,0:T(8,128)(2,1)S(1)}, bf16[256,256]{1,0:T(8,128)(2,1)}, u32[]{:S(2)}) copy-start(bf16[256,256]{1,0:T(8,128)(2,1)} %reshape.162) | copy-start | bytes 393220
  73.6 5.3 %copy-start.21 = (bf16[256,256]{1,0:T(8,128)(2,1)S(1)}, bf16[256,256]{1,0:T(8,128)(2,1)}, u32[]{:S(2)}) copy-start(bf16[256,256]{1,0:T(8,128)(2,1)} %reshape.163) | copy-start | bytes 393220
  75.1 4.0 %copy-start.23 = (bf16[256,256]{1,0:T(8,128)(2,1)S(1)}, bf16[256,256]{1,0:T(8,128)(2,1)}, u32[]{:S(2)}) copy-start(bf16[256,256]{1,0:T(8,128)(2,1)} %reshape.164) | copy-start | bytes 393220
  75.4 4.0 %copy-start.28 = (bf16[256,256]{1,0:T(8,128)(2,1)S(1)}, bf16[256,256]{1,0:T(8,128)(2,1)}, u32[]{:S(2)}) copy-start(bf16[256,256]{1,0:T(8,128)(2,1)} %reshape.165) | copy-start | bytes 393220
  75.6 5.3 %collective-permute-start.5 = (bf16[1,4,4,256]{3,2,1,0:T(4,128)(2,1)S(1)}, bf16[1,4,4,256]{3,2,1,0:T(4,128)(2,1)S(1)}, u32[]{:S(2)}, u32[]{:S(2)}) collective-permute-start(bf16[1,4,4,256]{3,2,1,0:T(4,128)(2,1)S(1)} %get-tuple-element.114), channel_id=1, source_target_pairs={{0,2},{1,3},{2,0},{3,1},{4,6},{5,7},{6,4},{7,5},{8,10},{9,11},{10,... | collective-permute-start | bytes 24584 | tf_op jit(solution)/shard_map/ppermute | solution.py:12
  77.7 3.7 %collective-permute-start.4 = (bf16[1,4,4,256]{3,2,1,0:T(4,128)(2,1)S(1)}, bf16[1,4,4,256]{3,2,1,0:T(4,128)(2,1)S(1)}, u32[]{:S(2)}, u32[]{:S(2)}) collective-permute-start(bf16[1,4,4,256]{3,2,1,0:T(4,128)(2,1)S(1)} %get-tuple-element.113), channel_id=1, source_target_pairs={{0,1},{1,0},{2,3},{3,2},{4,5},{5,4},{6,7},{7,6},{8,9},{9,8},{10,11... | collective-permute-start | bytes 24584 | tf_op jit(solution)/shard_map/ppermute | solution.py:12
  79.6 1.3 copy-start.7
  84.5 11.9 %copy-start.24 = (f32[256,256]{1,0:T(8,128)S(1)}, f32[256,256]{1,0:T(8,128)}, u32[]{:S(2)}) copy-start(f32[256,256]{1,0:T(8,128)} %fusion.29) | copy-start | bytes 786436
  96.4 3.7 %copy-start.29 = (bf16[256,256]{1,0:T(8,128)(2,1)S(1)}, bf16[256,256]{1,0:T(8,128)(2,1)}, u32[]{:S(2)}) copy-start(bf16[256,256]{1,0:T(8,128)(2,1)} %reshape.173) | copy-start | bytes 393220
  96.4 4.8 %copy-start.30 = (bf16[256,256]{1,0:T(8,128)(2,1)S(1)}, bf16[256,256]{1,0:T(8,128)(2,1)}, u32[]{:S(2)}) copy-start(bf16[256,256]{1,0:T(8,128)(2,1)} %reshape.174) | copy-start | bytes 393220
  96.4 6.0 %copy-start.31 = (bf16[256,256]{1,0:T(8,128)(2,1)S(1)}, bf16[256,256]{1,0:T(8,128)(2,1)}, u32[]{:S(2)}) copy-start(bf16[256,256]{1,0:T(8,128)(2,1)} %reshape.175) | copy-start | bytes 393220
  96.4 6.0 %copy-start.34 = (bf16[1,4,64,256]{3,2,1,0:T(8,128)(2,1)S(1)}, bf16[1,4,64,256]{3,2,1,0:T(8,128)(2,1)}, u32[]{:S(2)}) copy-start(bf16[1,4,64,256]{3,2,1,0:T(8,128)(2,1)} %param.10) | copy-start | bytes 393220
  109.4 1.8 copy-start.25
  111.6 1.1 copy-start.3
  112.3 1.1 copy-start.5
  112.7 1.1 copy-start.9
  114.2 0.8 copy-start.26
  256.0 2.4 copy-start.12
Sparse Core Ops, SparseCore 0:
  115.1 138.8 all-reduce.2
where the time goes:
time: 268 us; the launch traced here: 266 us
  waiting for transfers between devices  143 us (53%)
  local copies, waits for them, and re-layouts  52.9 us (20%)
  matrix products  24.8 us (9%)
  between operations  18.8 us (7%)
  other arithmetic  18.3 us (7%)
  starting transfers between devices  9.16 us (3%)
    psum x1, waiting for transfers between devices, on_device(): lax.psum((grad_one, grad_down, grad_two), ('scene', 'kd'))  139 us
    unnamed x90, local copies, waits for them, and re-layouts  12.5 us
    ppermute x6, starting transfers between devices, swapped(): return lax.ppermute(value, axis, pairs)  9.12 us
    dot_general x12, matrix products, conv_apply(): jnp.dot(taps[tap_index].reshape(-1, chans), weight[tap_index], preferred_...  7.73 us
    reshape x6, local copies, waits for them, and re-layouts, conv_apply(): taps[tap_index].reshape(-1, chans)  7.36 us
    dot_general x6, matrix products, conv_back(): lax.dot_general(taps[OPPOSITE[tap_index]].reshape(-1, chans), weight[tap_...  7.01 us
  transfers between devices with their start and end apart: 7, of which 3 were waited for; matrix products, arithmetic and copies ran while one was open for 3% of the time, Pallas kernels for 0%

commit v1 on v0

v1 whole, which is shorter than its diff:
```python
import functools

import jax
import jax.numpy as jnp
from jax import lax
from jax.experimental import pallas as pl
from jax.experimental.pallas import tpu as pltpu
from jax.sharding import PartitionSpec as P

MESH = pl.DeviceIdType.MESH
F32 = jnp.float32
BF16 = jnp.bfloat16
STRIDE = (16, 4, 1)
CLASS = (4, 2, 1)
OPPOSITE = (0, 2, 1, 4, 3, 6, 5)


def dot(a, b):
    return jnp.dot(a, b, preferred_element_type=F32)


def dot_tn(a, b):
    return lax.dot_general(a, b, (((0,), (0,)), ((), ())), preferred_element_type=F32)


def dot_nt(a, b):
    return lax.dot_general(a, b, (((1,), (1,)), ((), ())), preferred_element_type=F32)


def one_hot(mask):
    return jnp.where(mask, 1.0, 0.0).astype(BF16)


def sigmoid(v):
    return 0.5 * jnp.tanh(0.5 * v) + 0.5


def coordinate(row, axis):
    return (row // STRIDE[axis]) % 4


def face_rows(row, axis):
    first, second = [a for a in range(3) if a != axis]
    return coordinate(row, first) * 4 + coordinate(row, second)


def lanes(ref, classes):
    return jnp.concatenate([ref[:, c * 128 : (c + 1) * 128] for c in classes], axis=1)


class Reduction:
    def __init__(self, total, staged, landed, out, sems, bits, n_scene, n_kd):
        self.total, self.staged, self.landed, self.out = total, staged, landed, out
        self.send, self.recv = sems
        self.bits, self.n_kd = bits, n_kd
        self.piece = total.shape[0] // (n_scene * n_kd)
        self.scene = lax.axis_index("scene")
        self.kd = lax.axis_index("kd")
        self.sem = 0
        self.base = 0
        self.count = n_scene * n_kd
        self.offset = 0
        self.levels = []
        self.copies = []

    def rows(self, start, count):
        return pl.ds(pl.multiple_of(start * self.piece, 16), count * self.piece)

    def copy(self, src, dst, device):
        made = pltpu.make_async_remote_copy(
            src_ref=src,
            dst_ref=dst,
            send_sem=self.send.at[self.sem],
            recv_sem=self.recv.at[self.sem],
            device_id=device,
            device_id_type=MESH,
        )
        self.sem += 1
        made.start()
        return made

    def steps(self):
        for bit in self.bits:
            mask = 2**bit
            mine = (self.scene // mask) % 2
            half = self.count // 2
            other = {"scene": self.scene + mask - 2 * mask * mine}
            away = self.offset + (1 - mine) * half
            keep = self.offset + mine * half
            slot = pl.ds(self.base * self.piece, half * self.piece)
            self.staged[slot, :] = self.total[self.rows(away, half), :].astype(BF16)
            made = self.copy(self.staged.at[slot], self.landed.at[slot], other)
            yield
            made.wait()
            kept = self.rows(keep, half)
            self.total[kept, :] = self.total[kept, :] + self.landed[slot, :].astype(F32)
            self.base += half
            self.count = half
            self.offset = keep
            self.levels.append((other, keep, half))
        made = []
        for j in range(1, self.n_kd):
            peer = self.peer(j)
            slot = pl.ds(self.base * self.piece, self.piece)
            self.staged[slot, :] = self.total[self.rows(self.offset + peer, 1), :].astype(BF16)
            made.append((self.copy(self.staged.at[slot], self.landed.at[slot], {"kd": peer}), slot))
            self.base += 1
        yield
        own = self.rows(self.offset + self.kd, 1)
        value = self.total[own, :]
        for one, slot in made:
            one.wait()
            value = value + self.landed[slot, :].astype(F32)
        self.out[own, :] = value.astype(BF16)
        made = [
            self.copy(self.out.at[own], self.out.at[own], {"kd": self.peer(j)})
            for j in range(1, self.n_kd)
        ]
        yield
        for one in made:
            one.wait()
        for other, keep, half in reversed(self.levels):
            kept = self.rows(keep, half)
            one = self.copy(self.out.at[kept], self.out.at[kept], other)
            yield
            one.wait()

    def peer(self, j):
        result = self.kd
        bit = 1
        while bit < self.n_kd:
            if j & bit:
                result = result + bit - 2 * bit * ((self.kd // bit) % 2)
            bit *= 2
        return result


def kernel(
    n_scene,
    n_kd,
    n_bits,
    x_ref,
    send_ref,
    source_ref,
    cot_ref,
    w1_ref,
    dw_ref,
    w2_ref,
    enc_ref,
    out0_ref,
    out1_ref,
    xp_ref,
    t1_ref,
    slope_ref,
    patch_ref,
    shift_ref,
    place_ref,
    pick_ref,
    t2_ref,
    fs1,
    fr1,
    fs2,
    fr2,
    fs3,
    fr3,
    face_send,
    face_recv,
    tot0,
    stage0,
    land0,
    send0,
    recv0,
    tot1,
    stage1,
    land1,
    send1,
    recv1,
):
    bricks = source_ref.shape[0]
    rows = bricks * 64
    local = bricks * 6
    scene_bits = n_scene.bit_length() - 1
    kd = lax.axis_index("kd")
    scene = lax.axis_index("scene")
    order = list(range(scene_bits))
    sum0 = Reduction(tot0, stage0, land0, out0_ref, (send0, recv0), order, n_scene, n_kd)
    sum1 = Reduction(
        tot1, stage1, land1, out1_ref, (send1, recv1), order[:1] + order[:0:-1], n_scene, n_kd
    )

    barrier = pltpu.get_barrier_semaphore()
    for j in range(1, n_kd):
        pl.semaphore_signal(barrier, inc=1, device_id={"kd": sum0.peer(j)}, device_id_type=MESH)
    for bit in range(scene_bits):
        mask = 2**bit
        other = scene + mask - 2 * mask * ((scene // mask) % 2)
        pl.semaphore_signal(barrier, inc=1, device_id={"scene": other}, device_id_type=MESH)

    to = lax.broadcasted_iota(jnp.int32, (128, 128), 0)
    frm = lax.broadcasted_iota(jnp.int32, (128, 128), 1)
    wanted = (
        (to // 64) * 64
        + (2 * ((to // 4) % 4) + (to // 32) % 2) * 8
        + 2 * (to % 4)
        + (to // 16) % 2
    )
    arrange = one_hot(frm == wanted)
    for block in range(rows // 16):
        moved = dot(arrange, x_ref[block * 128 : (block + 1) * 128, :]).astype(BF16)
        for c in range(8):
            xp_ref[block * 16 : (block + 1) * 16, c * 128 : (c + 1) * 128] = moved[
                c * 16 : (c + 1) * 16
            ]

    face = lax.broadcasted_iota(jnp.int32, (16, rows), 0)
    voxel = lax.broadcasted_iota(jnp.int32, (16, rows), 1)
    for bit in range(n_bits):
        axis = bit % 3
        mine = (kd // 2**bit) % 2
        first, second = [a for a in range(3) if a != axis]
        at = (
            (send_ref[bit, 0] // 6) * 64
            + 3 * STRIDE[axis] * (1 - mine)
            + (face // 4) * STRIDE[first]
            + (face % 4) * STRIDE[second]
        )
        pick_ref[bit * 16 : (bit + 1) * 16, :] = one_hot(voxel == at)

    def exchange(stage, send_buf, recv_buf, pieces):
        copies = []
        for bit in range(n_bits):
            send_buf[bit] = pieces[bit].astype(BF16)
            made = pltpu.make_async_remote_copy(
                src_ref=send_buf.at[bit],
                dst_ref=recv_buf.at[bit],
                send_sem=face_send.at[stage * n_bits + bit],
                recv_sem=face_recv.at[stage * n_bits + bit],
                device_id={"kd": sum0.peer(2**bit)},
                device_id_type=MESH,
            )
            made.start()
            copies.append(made)
        return copies

    far = {}
    for axis in range(3):
        high = [c for c in range(8) if c & CLASS[axis]]
        low = [c for c in range(8) if not c & CLASS[axis]]
        far[2 * axis], far[2 * axis + 1] = high, low
    picked = dot(pick_ref[...], xp_ref[...])
    pieces = []
    for bit in range(n_bits):
        axis = bit % 3
        mine = (kd // 2**bit) % 2
        part = picked[bit * 16 : (bit + 1) * 16]
        pieces.append(
            jnp.where(mine == 0, lanes(part, far[2 * axis]), lanes(part, far[2 * axis + 1]))
        )
    pl.semaphore_wait(barrier, n_kd - 1 + scene_bits)
    copies = exchange(0, fs1, fr1, pieces)

    row = lax.broadcasted_iota(jnp.int32, (64, rows), 0)
    col = lax.broadcasted_iota(jnp.int32, (64, rows), 1)
    row16 = lax.broadcasted_iota(jnp.int32, (64, 16), 0)
    col16 = lax.broadcasted_iota(jnp.int32, (64, 16), 1)
    for s in range(6):
        axis, step = s // 2, STRIDE[s // 2]
        sign = 1 if s % 2 else -1
        edge = 3 if s % 2 else 0
        for b in range(bricks):
            source = source_ref[b, s]
            border = coordinate(row, axis) == edge
            base = jnp.where(source < local, (source // 6) * 64, -4096)
            at = row + jnp.where(border, base - sign * 3 * step, b * 64 + sign * step)
            shift_ref[s, b * 64 : (b + 1) * 64, :] = one_hot(col == at)
            for bit in range(axis, n_bits, 3):
                here = jnp.where(source == local + bit, 0, -4096)
                slot = jnp.where(
                    coordinate(row16, axis) == edge, face_rows(row16, axis) + here, -4096
                )
                place_ref[bit, s % 2, b * 64 : (b + 1) * 64, :] = one_hot(col16 == slot)

    def shifted(s, operand, arrived):
        value = dot(shift_ref[s], operand)
        for bit in range(s // 2, n_bits, 3):
            value = value + dot(place_ref[bit, s % 2], arrived[bit])
        return value.astype(BF16)

    sides = sorted(range(6), key=lambda s: (s // 2 < n_bits, s))

    for c in range(8):
        t1_ref[c, :, 0:128] = xp_ref[:, c * 128 : (c + 1) * 128]
    for s in range(6):
        tap = slice((s + 1) * 128, (s + 2) * 128)
        for c in far[s]:
            near = c ^ CLASS[s // 2]
            t1_ref[c, :, tap] = xp_ref[:, near * 128 : (near + 1) * 128]
    waited = False
    for s in sides:
        if s // 2 < n_bits and not waited:
            for made in copies:
                made.wait()
            waited = True
        tap = slice((s + 1) * 128, (s + 2) * 128)
        moved = shifted(s, lanes(xp_ref, far[s]), fr1)
        for k, c in enumerate(far[s]):
            t1_ref[c ^ CLASS[s // 2], :, tap] = moved[:, k * 128 : (k + 1) * 128]

    for c in range(8):
        cols = slice(c * 128, (c + 1) * 128)
        pre = dot(t1_ref[c], w1_ref[...])
        g = sigmoid(pre)
        slope_ref[:, cols] = g * (1.0 + pre * (1.0 - g))
        patch_ref[:, cols] = (xp_ref[:, cols].astype(F32) + pre * g).astype(BF16)

    coarse = dot(patch_ref[...], dw_ref[...]).astype(BF16)
    picked = dot(pick_ref[...], coarse)
    copies = exchange(1, fs2, fr2, [picked[i * 16 : (i + 1) * 16] for i in range(n_bits)])
    t2_ref[:, 0:256] = coarse
    waited = False
    for s in sides:
        if s // 2 < n_bits and not waited:
            for made in copies:
                made.wait()
            waited = True
        t2_ref[:, (s + 1) * 256 : (s + 2) * 256] = shifted(s, coarse, fr2)
    pre = dot(t2_ref[...], w2_ref[...])
    g = sigmoid(pre)
    enc_ref[...] = (coarse.astype(F32) + pre * g).astype(BF16)
    upstream = cot_ref[...].astype(F32)
    delta = (upstream * (g * (1.0 + pre * (1.0 - g)))).astype(BF16)
    picked = dot(pick_ref[...], delta)
    copies = exchange(2, fs3, fr3, [picked[i * 16 : (i + 1) * 16] for i in range(n_bits)])

    wide = 7 * 256
    grad_two = dot_tn(t2_ref[...], delta)
    tot0[0:wide, :] = grad_two[:, 0:128]
    tot0[wide : 2 * wide, :] = grad_two[:, 128:256]
    if tot0.shape[0] > 2 * wide:
        tot0[2 * wide :, :] = jnp.zeros((tot0.shape[0] - 2 * wide, 128), F32)
    run0 = sum0.steps()
    next(run0)

    back = upstream + dot_nt(delta, w2_ref[0:256, :])
    waited = False
    for s in sides:
        if s // 2 < n_bits and not waited:
            for made in copies:
                made.wait()
            waited = True
        t = OPPOSITE[s + 1]
        back = back + dot_nt(shifted(s, delta, fr3), w2_ref[t * 256 : (t + 1) * 256, :])
    grad_coarse = back.astype(BF16)
    next(run0)

    high = 8 * 128
    grad_down = dot_tn(patch_ref[...], grad_coarse)
    tot1[0:high, :] = grad_down[:, 0:128]
    tot1[high : 2 * high, :] = grad_down[:, 128:256]
    grad_one = jnp.zeros((7 * 128, 128), F32)
    for c in range(8):
        cols = slice(c * 128, (c + 1) * 128)
        patch_grad = dot_nt(grad_coarse, dw_ref[cols, :])
        delta_one = (patch_grad * slope_ref[:, cols]).astype(BF16)
        grad_one = grad_one + dot_tn(t1_ref[c], delta_one)
    end = 2 * high + 7 * 128
    tot1[2 * high : end, :] = grad_one
    if tot1.shape[0] > end:
        tot1[end:, :] = jnp.zeros((tot1.shape[0] - end, 128), F32)
    run1 = sum1.steps()
    next(run1)
    pending = [run0, run1]
    while pending:
        for run in list(pending):
            if next(run, "end") == "end":
                pending.remove(run)


def padded(rows, devices):
    return -(-rows // (16 * devices)) * 16 * devices


def on_device(n_scene, n_kd, features, send_faces, face_source, cotangent, conv_one, down, conv_two):
    bricks = features.shape[1]
    n_bits = send_faces.shape[2]
    rows = bricks * 64
    devices = n_scene * n_kd
    scene_bits = n_scene.bit_length() - 1
    size0 = padded(2 * 7 * 256, devices)
    size1 = padded(2 * 1024 + 7 * 128, devices)
    n_sems = 2 * scene_bits + 2 * (n_kd - 1)
    vmem = pl.BlockSpec(memory_space=pltpu.VMEM)
    smem = pl.BlockSpec(memory_space=pltpu.SMEM)

    def reduction(size):
        return [
            pltpu.VMEM((size, 128), F32),
            pltpu.VMEM((size, 128), BF16),
            pltpu.VMEM((size, 128), BF16),
            pltpu.SemaphoreType.DMA((n_sems,)),
            pltpu.SemaphoreType.DMA((n_sems,)),
        ]

    encoded, sum0, sum1 = pl.pallas_call(
        functools.partial(kernel, n_scene, n_kd, n_bits),
        out_shape=(
            jax.ShapeDtypeStruct((rows, 256), BF16),
            jax.ShapeDtypeStruct((size0, 128), BF16),
            jax.ShapeDtypeStruct((size1, 128), BF16),
        ),
        in_specs=[vmem, smem, smem, vmem, vmem, vmem, vmem],
        out_specs=(vmem, vmem, vmem),
        scratch_shapes=[
            pltpu.VMEM((rows, 1024), BF16),
            pltpu.VMEM((8, rows, 7 * 128), BF16),
            pltpu.VMEM((rows, 1024), F32),
            pltpu.VMEM((rows, 1024), BF16),
            pltpu.VMEM((6, rows, rows), BF16),
            pltpu.VMEM((n_bits, 2, rows, 16), BF16),
            pltpu.VMEM((n_bits * 16, rows), BF16),
            pltpu.VMEM((rows, 7 * 256), BF16),
            pltpu.VMEM((n_bits, 16, 512), BF16),
            pltpu.VMEM((n_bits, 16, 512), BF16),
            pltpu.VMEM((n_bits, 16, 256), BF16),
            pltpu.VMEM((n_bits, 16, 256), BF16),
            pltpu.VMEM((n_bits, 16, 256), BF16),
            pltpu.VMEM((n_bits, 16, 256), BF16),
            pltpu.SemaphoreType.DMA((3 * n_bits,)),
            pltpu.SemaphoreType.DMA((3 * n_bits,)),
        ]
        + reduction(size0)
        + reduction(size1),
        compiler_params=pltpu.CompilerParams(
            collective_id=0, has_side_effects=True, vmem_limit_bytes=48 * 2**20
        ),
    )(
        features.reshape(bricks * 512, 128),
        send_faces[0, 0],
        face_source[0],
        cotangent.reshape(rows, 256),
        conv_one.reshape(7 * 128, 128),
        down,
        conv_two.reshape(7 * 256, 256),
    )
    wide = 7 * 256
    grad_two = jnp.concatenate([sum0[:wide], sum0[wide : 2 * wide]], axis=1).astype(F32)
    grad_down = jnp.concatenate([sum1[:1024], sum1[1024:2048]], axis=1).astype(F32)
    grad_one = sum1[2048 : 2048 + 7 * 128].astype(F32)
    return (
        encoded.reshape(1, bricks, 64, 256),
        grad_one.reshape(7, 128, 128),
        grad_down,
        grad_two.reshape(7, 256, 256),
    )


def solution(mesh):
    placed = (
        P("scene", "kd", None, None),
        P("scene", "kd", None, None),
        P("scene", "kd", None),
        P("scene", "kd", None, None),
        P(),
        P(),
        P(),
    )
    return jax.shard_map(
        functools.partial(on_device, mesh.shape["scene"], mesh.shape["kd"]),
        mesh=mesh,
        in_specs=placed,
        out_specs=(P("scene", "kd", None, None), P(), P(), P()),
        check_vma=False,
    )
```

time: 268 us -> 68.3 us (0.25)
  waiting for transfers between devices: 143 us -> 0 us
  Pallas kernels: 0 us -> 56.8 us
  local copies, waits for them, and re-layouts: 52.9 us -> 7.29 us
  matrix products: 24.8 us -> 0 us
  between operations: 18.8 us -> 0.67 us
  other arithmetic: 18.3 us -> 3.19 us
  starting transfers between devices: 9.16 us -> 0 us
    psum x1 -> x0, waiting for transfers between devices: 139 us -> none  [on_device(): lax.psum((grad_one, grad_down, grad_two), ('scene', 'kd'))]
    pallas_call x0 -> x1, Pallas kernels: none -> 56.8 us  [on_device(): pl.pallas_call(functools.partial(kernel, n_scene, n_kd, n_bits), out_shap...]
    dot_general x38 -> x0, matrix products: 24.8 us -> none  [the longest x12 7.73 us: conv_apply(): jnp.dot(taps[tap_index].reshape(-1, chans), weight[tap_index], preferred_...]
    reshape x18 -> x0, local copies, waits for them, and re-layouts: 19.1 us -> none  [the longest x6 7.36 us: conv_apply(): taps[tap_index].reshape(-1, chans)]
    concatenate x18 -> x0, other arithmetic: 17.9 us -> none  [the longest x3 3.29 us: shift_taps(): jnp.concatenate([border[:, 4][:, :, :, None], blocks[:, :, :, :-1]], 3)]
    slice x13 -> x3, local copies, waits for them, and re-layouts: 11 us -> 0.11 us  [the longest x1 0.06 us: on_device(): sum0[:wide]]
    ppermute x6 -> x0, starting transfers between devices: 9.12 us -> none  [swapped(): return lax.ppermute(value, axis, pairs)]
    another operation x15 -> x0, local copies, waits for them, and re-layouts: 6.86 us -> none  [the longest x5 3.3 us: shift_taps(): border[:, 5][:, :, :, None]]
  transfers between devices with their start and end apart: 7 -> 0, of which waited for: 3 -> 0; matrix products, arithmetic and copies ran while one was open for 3% -> 0% of each run, Pallas kernels for 0% -> 0%
where the time goes in v1:
time: 68.3 us; the launch traced here: 68 us
  Pallas kernels  56.8 us (83%)
  local copies, waits for them, and re-layouts  7.29 us (11%)
  other arithmetic  3.19 us (5%)
    pallas_call x1, Pallas kernels, on_device(): pl.pallas_call(functools.partial(kernel, n_scene, n_kd, n_bits), out_shap...  56.8 us
    unnamed x13, local copies, waits for them, and re-layouts  6.44 us

profile of v1, /device:TPU:0, one launch (start us, length us, event | category | flops | bytes accessed | tf_op | source)
XLA Modules:
  0.0 68.0 jit_solution(1372251635168690184)
XLA Ops:
  0.6 0.7 %copy.11.send_ref = s32[2,1]{1,0:T(2,128)S(1)} copy(s32[2,1]{0,1:T(1,128)} %bitcast.20) | data formatting | bytes 16 | tf_op jit(solution)/shard_map/squeeze | solution.py:438
  1.4 0.0 copy-start
  1.4 1.2 %copy-done = bf16[7,256,256]{2,1,0:T(8,128)(2,1)S(1)} copy-done((bf16[7,256,256]{2,1,0:T(8,128)(2,1)S(1)}, bf16[7,256,256]{2,1,0:T(8,128)(2,1)}, u32[]{:S(2)}) %copy-start) | copy-done | bytes 917528
  2.6 0.0 copy-start.1
  2.6 1.0 %copy-done.1 = bf16[1,4,512,128]{3,2,1,0:T(8,128)(2,1)S(1)} copy-done((bf16[1,4,512,128]{3,2,1,0:T(8,128)(2,1)S(1)}, bf16[1,4,512,128]{3,2,1,0:T(8,128)(2,1)}, u32[]{:S(2)}) %copy-start.1) | copy-done | bytes 524312
  3.6 0.0 copy-start.2
  3.6 1.0 %copy-done.2 = bf16[1024,256]{1,0:T(8,128)(2,1)S(1)} copy-done((bf16[1024,256]{1,0:T(8,128)(2,1)S(1)}, bf16[1024,256]{1,0:T(8,128)(2,1)}, u32[]{:S(2)}) %copy-start.2) | copy-done | bytes 524312
  4.6 0.0 copy-start.3
  4.6 0.9 %copy-done.3 = bf16[7,128,128]{2,1,0:T(8,128)(2,1)S(1)} copy-done((bf16[7,128,128]{2,1,0:T(8,128)(2,1)S(1)}, bf16[7,128,128]{2,1,0:T(8,128)(2,1)}, u32[]{:S(2)}) %copy-start.3) | copy-done | bytes 229400
  5.6 0.0 copy-start.4
  5.6 0.9 %copy-done.4 = bf16[1,4,64,256]{3,2,1,0:T(8,128)(2,1)S(1)} copy-done((bf16[1,4,64,256]{3,2,1,0:T(8,128)(2,1)S(1)}, bf16[1,4,64,256]{3,2,1,0:T(8,128)(2,1)}, u32[]{:S(2)}) %copy-start.4) | copy-done | bytes 131096
  6.5 0.0 copy-start.5
  6.5 0.7 copy-done.5
  7.2 56.8 %shard_map.102 = (bf16[256,256]{1,0:T(8,128)(2,1)S(1)}, bf16[3584,128]{1,0:T(8,128)(2,1)S(1)}, bf16[3072,128]{1,0:T(8,128)(2,1)S(1)}) custom-call(bf16[2048,128]{1,0:T(8,128)(2,1)S(1)} %bitcast.12, s32[2,1]{1,0:T(2,128)S(1)} %copy.11.send_ref, s32[4,6]{1,0:T(4,128)S(1)} %bitcast.16, bf16[256,256]{1,0:T(8,128)(2,1)S(1)} %bitcast.14, ...), custom_call_target="tpu_custom_call" | custom-call | tf_op jit(solution)/shard_map/pallas_call | solution.py:404
  64.1 0.8 %convert.1 = f32[7,128,128]{2,1,0:T(8,128)} convert(bf16[7,128,128]{2,1,0:T(8,128)(2,1)S(1)} %bitcast.19) | non-fusion elementwise | flops 114688 | bytes 688128 | tf_op jit(solution)/shard_map/reshape | solution.py:451
  64.9 1.0 %maximum_convert_fusion.1 = f32[1024,256]{1,0:T(8,128)} fusion(bf16[1024,128]{1,0:T(8,128)(2,1)S(1)} %get-tuple-element.13, bf16[1024,128]{1,0:T(8,128)(2,1)S(1)} %get-tuple-element.12), kind=kLoop, calls=%fused_computation.1 | loop fusion | flops 1048576 | bytes 1572864 | tf_op jit(solution)/shard_map/convert_element_type | solution.py:447
  65.9 0.1 fusion
  66.0 1.3 %maximum_convert_fusion = f32[7,256,256]{2,1,0:T(8,128)} fusion(bf16[7,256,128]{2,1,0:T(8,128)(2,1)S(1)} %bitcast.18, bf16[7,256,128]{2,1,0:T(8,128)(2,1)S(1)} %bitcast.17), kind=kLoop, calls=%fused_computation | loop fusion | flops 1835008 | bytes 2752512 | tf_op jit(solution)/shard_map/convert_element_type | solution.py:446
  67.3 0.7 copy.13
  (2 shorter events, 0.1 us)
Async XLA Ops:
  1.4 1.2 %copy-start = (bf16[7,256,256]{2,1,0:T(8,128)(2,1)S(1)}, bf16[7,256,256]{2,1,0:T(8,128)(2,1)}, u32[]{:S(2)}) copy-start(bf16[7,256,256]{2,1,0:T(8,128)(2,1)} %param.13) | copy-start | bytes 2752516
  2.6 1.0 %copy-start.1 = (bf16[1,4,512,128]{3,2,1,0:T(8,128)(2,1)S(1)}, bf16[1,4,512,128]{3,2,1,0:T(8,128)(2,1)}, u32[]{:S(2)}) copy-start(bf16[1,4,512,128]{3,2,1,0:T(8,128)(2,1)} %param.7) | copy-start | bytes 1572868
  3.6 1.0 %copy-start.2 = (bf16[1024,256]{1,0:T(8,128)(2,1)S(1)}, bf16[1024,256]{1,0:T(8,128)(2,1)}, u32[]{:S(2)}) copy-start(bf16[1024,256]{1,0:T(8,128)(2,1)} %dw_ref.1) | copy-start | bytes 1572868
  4.6 0.9 %copy-start.3 = (bf16[7,128,128]{2,1,0:T(8,128)(2,1)S(1)}, bf16[7,128,128]{2,1,0:T(8,128)(2,1)}, u32[]{:S(2)}) copy-start(bf16[7,128,128]{2,1,0:T(8,128)(2,1)} %param.11) | copy-start | bytes 688132
  5.6 0.9 %copy-start.4 = (bf16[1,4,64,256]{3,2,1,0:T(8,128)(2,1)S(1)}, bf16[1,4,64,256]{3,2,1,0:T(8,128)(2,1)}, u32[]{:S(2)}) copy-start(bf16[1,4,64,256]{3,2,1,0:T(8,128)(2,1)} %param.10) | copy-start | bytes 393220
  6.5 0.7 %copy-start.5 = (s32[1,4,6]{2,1,0:T(4,128)S(1)}, s32[1,4,6]{2,1,0:T(4,128)}, u32[]{:S(2)}) copy-start(s32[1,4,6]{2,1,0:T(4,128)} %param.9) | copy-start | bytes 292

commit v2 on v1

--- a/solution.py
+++ b/solution.py
@@ -135,62 +135,46 @@
         return result
 
 
-def kernel(
-    n_scene,
-    n_kd,
-    n_bits,
-    x_ref,
-    send_ref,
-    source_ref,
-    cot_ref,
-    w1_ref,
-    dw_ref,
-    w2_ref,
-    enc_ref,
-    out0_ref,
-    out1_ref,
-    xp_ref,
-    t1_ref,
-    slope_ref,
-    patch_ref,
-    shift_ref,
-    place_ref,
-    pick_ref,
-    t2_ref,
-    fs1,
-    fr1,
-    fs2,
-    fr2,
-    fs3,
-    fr3,
-    face_send,
-    face_recv,
-    tot0,
-    stage0,
-    land0,
-    send0,
-    recv0,
-    tot1,
-    stage1,
-    land1,
-    send1,
-    recv1,
-):
-    bricks = source_ref.shape[0]
+def kernel(n_scene, n_kd, n_bits, *refs):
+    refs = list(refs)
+
+    def take(count):
+        taken = refs[:count]
+        del refs[:count]
+        return taken
+
+    x_hbm, send_ref, source_ref, cot_hbm, w1_hbm, dw_hbm, w2_hbm = take(7)
+    enc_ref, *outs = take(5)
+    x_ref, cot_ref, w1_ref, dw_ref, w2_ref, in_sem = take(6)
+    xp_ref, t1_ref, t1t_ref, slope_ref, patch_ref, patcht_ref, delta1_ref = take(7)
+    shift_ref, place_ref, pick_ref, t2_ref, td_ref = take(5)
+    fs1, fr1, fs2, fr2, fs3, fr3, face_send, face_recv = take(8)
+    bricks = source_ref.shape[1]
     rows = bricks * 64
     local = bricks * 6
     scene_bits = n_scene.bit_length() - 1
     kd = lax.axis_index("kd")
     scene = lax.axis_index("scene")
-    order = list(range(scene_bits))
-    sum0 = Reduction(tot0, stage0, land0, out0_ref, (send0, recv0), order, n_scene, n_kd)
-    sum1 = Reduction(
-        tot1, stage1, land1, out1_ref, (send1, recv1), order[:1] + order[:0:-1], n_scene, n_kd
-    )
+    up = list(range(scene_bits))
+    chains = []
+    for k in range(4):
+        total, staged, landed, send, recv = take(5)
+        order = up if k % 2 == 0 else up[:1] + up[:0:-1]
+        chains.append(
+            Reduction(total, staged, landed, outs[k], (send, recv), order, n_scene, n_kd)
+        )
+    loads = []
+    for k, (src, dst) in enumerate(
+        ((x_hbm, x_ref), (w1_hbm, w1_ref), (dw_hbm, dw_ref), (w2_hbm, w2_ref), (cot_hbm, cot_ref))
+    ):
+        loads.append(pltpu.make_async_copy(src, dst, in_sem.at[k]))
+        loads[-1].start()
+    load_x, load_w1, load_dw, load_w2, load_cot = loads
 
     barrier = pltpu.get_barrier_semaphore()
     for j in range(1, n_kd):
-        pl.semaphore_signal(barrier, inc=1, device_id={"kd": sum0.peer(j)}, device_id_type=MESH)
+        peer = chains[0].peer(j)
+        pl.semaphore_signal(barrier, inc=1, device_id={"kd": peer}, device_id_type=MESH)
     for bit in range(scene_bits):
         mask = 2**bit
         other = scene + mask - 2 * mask * ((scene // mask) % 2)
@@ -205,12 +189,6 @@
         + (to // 16) % 2
     )
     arrange = one_hot(frm == wanted)
-    for block in range(rows // 16):
-        moved = dot(arrange, x_ref[block * 128 : (block + 1) * 128, :]).astype(BF16)
-        for c in range(8):
-            xp_ref[block * 16 : (block + 1) * 16, c * 128 : (c + 1) * 128] = moved[
-                c * 16 : (c + 1) * 16
-            ]
 
     face = lax.broadcasted_iota(jnp.int32, (16, rows), 0)
     voxel = lax.broadcasted_iota(jnp.int32, (16, rows), 1)
@@ -219,12 +197,20 @@
         mine = (kd // 2**bit) % 2
         first, second = [a for a in range(3) if a != axis]
         at = (
-            (send_ref[bit, 0] // 6) * 64
+            (send_ref[0, bit] // 6) * 64
             + 3 * STRIDE[axis] * (1 - mine)
             + (face // 4) * STRIDE[first]
             + (face % 4) * STRIDE[second]
         )
         pick_ref[bit * 16 : (bit + 1) * 16, :] = one_hot(voxel == at)
+
+    load_x.wait()
+    for block in range(rows // 16):
+        moved = dot(arrange, x_ref[block * 128 : (block + 1) * 128, :]).astype(BF16)
+        for c in range(8):
+            xp_ref[block * 16 : (block + 1) * 16, c * 128 : (c + 1) * 128] = moved[
+                c * 16 : (c + 1) * 16
+            ]
 
     def exchange(stage, send_buf, recv_buf, pieces):
         copies = []
@@ -235,7 +221,7 @@
                 dst_ref=recv_buf.at[bit],
                 send_sem=face_send.at[stage * n_bits + bit],
                 recv_sem=face_recv.at[stage * n_bits + bit],
-                device_id={"kd": sum0.peer(2**bit)},
+                device_id={"kd": chains[0].peer(2**bit)},
                 device_id_type=MESH,
             )
             made.start()
@@ -244,9 +230,8 @@
 
     far = {}
     for axis in range(3):
-        high = [c for c in range(8) if c & CLASS[axis]]
-        low = [c for c in range(8) if not c & CLASS[axis]]
-        far[2 * axis], far[2 * axis + 1] = high, low
+        far[2 * axis] = [c for c in range(8) if c & CLASS[axis]]
+        far[2 * axis + 1] = [c for c in range(8) if not c & CLASS[axis]]
     picked = dot(pick_ref[...], xp_ref[...])
     pieces = []
     for bit in range(n_bits):
@@ -266,64 +251,66 @@
     for s in range(6):
         axis, step = s // 2, STRIDE[s // 2]
         sign = 1 if s % 2 else -1
-        edge = 3 if s % 2 else 0
+        border = coordinate(row, axis) == (3 if s % 2 else 0)
+        border16 = coordinate(row16, axis) == (3 if s % 2 else 0)
+        gap = col - row
+        gap16 = col16 - face_rows(row16, axis)
         for b in range(bricks):
-            source = source_ref[b, s]
-            border = coordinate(row, axis) == edge
+            source = source_ref[0, b, s]
             base = jnp.where(source < local, (source // 6) * 64, -4096)
-            at = row + jnp.where(border, base - sign * 3 * step, b * 64 + sign * step)
-            shift_ref[s, b * 64 : (b + 1) * 64, :] = one_hot(col == at)
+            wish = jnp.where(border, base - sign * 3 * step, b * 64 + sign * step)
+            shift_ref[s, b * 64 : (b + 1) * 64, :] = one_hot(gap == wish)
             for bit in range(axis, n_bits, 3):
                 here = jnp.where(source == local + bit, 0, -4096)
-                slot = jnp.where(
-                    coordinate(row16, axis) == edge, face_rows(row16, axis) + here, -4096
-                )
-                place_ref[bit, s % 2, b * 64 : (b + 1) * 64, :] = one_hot(col16 == slot)
-
-    def shifted(s, operand, arrived):
-        value = dot(shift_ref[s], operand)
-        for bit in range(s // 2, n_bits, 3):
-            value = value + dot(place_ref[bit, s % 2], arrived[bit])
-        return value.astype(BF16)
-
-    sides = sorted(range(6), key=lambda s: (s // 2 < n_bits, s))
+                wish = jnp.where(border16, here, -4096)
+                place_ref[bit, s % 2, b * 64 : (b + 1) * 64, :] = one_hot(gap16 == wish)
 
     for c in range(8):
         t1_ref[c, :, 0:128] = xp_ref[:, c * 128 : (c + 1) * 128]
     for s in range(6):
         tap = slice((s + 1) * 128, (s + 2) * 128)
-        for c in far[s]:
+        moved = dot(shift_ref[s], lanes(xp_ref, far[s])).astype(BF16)
+        for k, c in enumerate(far[s]):
             near = c ^ CLASS[s // 2]
             t1_ref[c, :, tap] = xp_ref[:, near * 128 : (near + 1) * 128]
-    waited = False
-    for s in sides:
-        if s // 2 < n_bits and not waited:
-            for made in copies:
-                made.wait()
-            waited = True
-        tap = slice((s + 1) * 128, (s + 2) * 128)
-        moved = shifted(s, lanes(xp_ref, far[s]), fr1)
-        for k, c in enumerate(far[s]):
-            t1_ref[c ^ CLASS[s // 2], :, tap] = moved[:, k * 128 : (k + 1) * 128]
-
+            t1_ref[near, :, tap] = moved[:, k * 128 : (k + 1) * 128]
+    for made in copies:
+        made.wait()
+    for bit in range(n_bits):
+        for s in (2 * (bit % 3), 2 * (bit % 3) + 1):
+            tap = slice((s + 1) * 128, (s + 2) * 128)
+            moved = dot(place_ref[bit, s % 2], fr1[bit]).astype(BF16)
+            for k, c in enumerate(far[s]):
+                near = c ^ CLASS[s // 2]
+                t1_ref[near, :, tap] = t1_ref[near, :, tap] + moved[:, k * 128 : (k + 1) * 128]
+
+    load_w1.wait()
+    pre_one = dot(t1_ref[...].reshape(8 * rows, 7 * 128), w1_ref[...])
     for c in range(8):
         cols = slice(c * 128, (c + 1) * 128)
-        pre = dot(t1_ref[c], w1_ref[...])
+        pre = pre_one[c * rows : (c + 1) * rows]
         g = sigmoid(pre)
         slope_ref[:, cols] = g * (1.0 + pre * (1.0 - g))
         patch_ref[:, cols] = (xp_ref[:, cols].astype(F32) + pre * g).astype(BF16)
 
+    load_dw.wait()
     coarse = dot(patch_ref[...], dw_ref[...]).astype(BF16)
     picked = dot(pick_ref[...], coarse)
     copies = exchange(1, fs2, fr2, [picked[i * 16 : (i + 1) * 16] for i in range(n_bits)])
     t2_ref[:, 0:256] = coarse
-    waited = False
-    for s in sides:
-        if s // 2 < n_bits and not waited:
-            for made in copies:
-                made.wait()
-            waited = True
-        t2_ref[:, (s + 1) * 256 : (s + 2) * 256] = shifted(s, coarse, fr2)
+    for s in range(6):
+        t2_ref[:, (s + 1) * 256 : (s + 2) * 256] = dot(shift_ref[s], coarse).astype(BF16)
+    for c in range(8):
+        t1t_ref[:, c * rows : (c + 1) * rows] = t1_ref[c].T
+        patcht_ref[c * 128 : (c + 1) * 128, :] = patch_ref[:, c * 128 : (c + 1) * 128].T
+    for made in copies:
+        made.wait()
+    for bit in range(n_bits):
+        for s in (2 * (bit % 3), 2 * (bit % 3) + 1):
+            tap = slice((s + 1) * 256, (s + 2) * 256)
+            t2_ref[:, tap] = t2_ref[:, tap] + dot(place_ref[bit, s % 2], fr2[bit]).astype(BF16)
+    load_w2.wait()
+    load_cot.wait()
     pre = dot(t2_ref[...], w2_ref[...])
     g = sigmoid(pre)
     enc_ref[...] = (coarse.astype(F32) + pre * g).astype(BF16)
@@ -332,48 +319,103 @@
     picked = dot(pick_ref[...], delta)
     copies = exchange(2, fs3, fr3, [picked[i * 16 : (i + 1) * 16] for i in range(n_bits)])
 
-    wide = 7 * 256
     grad_two = dot_tn(t2_ref[...], delta)
-    tot0[0:wide, :] = grad_two[:, 0:128]
-    tot0[wide : 2 * wide, :] = grad_two[:, 128:256]
-    if tot0.shape[0] > 2 * wide:
-        tot0[2 * wide :, :] = jnp.zeros((tot0.shape[0] - 2 * wide, 128), F32)
-    run0 = sum0.steps()
-    next(run0)
-
-    back = upstream + dot_nt(delta, w2_ref[0:256, :])
-    waited = False
-    for s in sides:
-        if s // 2 < n_bits and not waited:
-            for made in copies:
-                made.wait()
-            waited = True
+    flat = jnp.concatenate([grad_two[:, 0:128], grad_two[:, 128:256]], axis=0)
+    fill(chains[0].total, flat[0:CUT])
+    fill(chains[1].total, flat[CUT:])
+    runs = [chains[0].steps(), chains[1].steps()]
+    pump(runs)
+
+    td_ref[:, 0:256] = delta
+    for s in range(6):
         t = OPPOSITE[s + 1]
-        back = back + dot_nt(shifted(s, delta, fr3), w2_ref[t * 256 : (t + 1) * 256, :])
+        td_ref[:, t * 256 : (t + 1) * 256] = dot(shift_ref[s], delta).astype(BF16)
+    for made in copies:
+        made.wait()
+    for bit in range(n_bits):
+        for s in (2 * (bit % 3), 2 * (bit % 3) + 1):
+            t = OPPOSITE[s + 1]
+            tap = slice(t * 256, (t + 1) * 256)
+            td_ref[:, tap] = td_ref[:, tap] + dot(place_ref[bit, s % 2], fr3[bit]).astype(BF16)
+    pump(runs)
+    back = upstream
+    for t in range(7):
+        tap = slice(t * 256, (t + 1) * 256)
+        back = back + dot_nt(td_ref[:, tap], w2_ref[tap, :])
     grad_coarse = back.astype(BF16)
-    next(run0)
-
-    high = 8 * 128
-    grad_down = dot_tn(patch_ref[...], grad_coarse)
-    tot1[0:high, :] = grad_down[:, 0:128]
-    tot1[high : 2 * high, :] = grad_down[:, 128:256]
-    grad_one = jnp.zeros((7 * 128, 128), F32)
+
+    grad_down = dot(patcht_ref[...], grad_coarse)
+    fill(
+        chains[2].total, jnp.concatenate([grad_down[:, 0:128], grad_down[:, 128:256]], axis=0)
+    )
+    pump(runs)
+    runs.append(chains[2].steps())
+    pump(runs[2:])
     for c in range(8):
         cols = slice(c * 128, (c + 1) * 128)
         patch_grad = dot_nt(grad_coarse, dw_ref[cols, :])
-        delta_one = (patch_grad * slope_ref[:, cols]).astype(BF16)
-        grad_one = grad_one + dot_tn(t1_ref[c], delta_one)
-    end = 2 * high + 7 * 128
-    tot1[2 * high : end, :] = grad_one
-    if tot1.shape[0] > end:
-        tot1[end:, :] = jnp.zeros((tot1.shape[0] - end, 128), F32)
-    run1 = sum1.steps()
-    next(run1)
-    pending = [run0, run1]
-    while pending:
-        for run in list(pending):
-            if next(run, "end") == "end":
-                pending.remove(run)
+        delta1_ref[c * rows : (c + 1) * rows, :] = (patch_grad * slope_ref[:, cols]).astype(BF16)
+    pump(runs)
+    fill(chains[3].total, dot(t1t_ref[...], delta1_ref[...]))
+    runs.append(chains[3].steps())
+    pump(runs[3:])
+    while runs:
+        pump(runs)
+
+
+CUT = 2048
+
+
+def fill(ref, value):
+    ref[0 : value.shape[0], :] = value
+    if ref.shape[0] > value.shape[0]:
+        ref[value.shape[0] :, :] = jnp.zeros((ref.shape[0] - value.shape[0], 128), F32)
+
+
+def pump(runs):
+    for run in list(runs):
+        if next(run, "end") == "end":
+            runs.remove(run)
+
+
+def finish(*refs):
+    incoming, (enc_out, one_out, down_out, two_out), held = refs[:5], refs[5:9], refs[9:14]
+    one_ref, down_ref, two_ref, load_sems, sems = refs[14:]
+    loads = [
+        pltpu.make_async_copy(src, dst, load_sems.at[k])
+        for k, (src, dst) in enumerate(zip(incoming, held))
+    ]
+    for k in (0, 1, 2, 3, 4):
+        loads[k].start()
+    a_ref, b_ref, c_ref, d_ref, enc_ref = held
+    copies = []
+
+    def send(src, dst):
+        copies.append(pltpu.make_async_copy(src, dst, sems.at[len(copies)]))
+        copies[-1].start()
+
+    loads[0].wait()
+    loads[1].wait()
+    for t in range(7):
+        at = slice(t * 256, (t + 1) * 256)
+        two_ref[at, 0:128] = a_ref[at, :].astype(F32)
+        low = 1792 + t * 256
+        right = a_ref[low : low + 256, :] if low < CUT else b_ref[low - CUT : low - CUT + 256, :]
+        two_ref[at, 128:256] = right.astype(F32)
+        send(two_ref.at[at], two_out.at[at])
+    loads[2].wait()
+    for part in range(4):
+        at = slice(part * 256, (part + 1) * 256)
+        down_ref[at, 0:128] = c_ref[at, :].astype(F32)
+        down_ref[at, 128:256] = c_ref[1024 + part * 256 : 1280 + part * 256, :].astype(F32)
+        send(down_ref.at[at], down_out.at[at])
+    loads[3].wait()
+    one_ref[...] = d_ref[0:896, :].astype(F32)
+    send(one_ref, one_out)
+    loads[4].wait()
+    send(enc_ref, enc_out)
+    for one in copies:
+        one.wait()
 
 
 def padded(rows, devices):
@@ -386,11 +428,11 @@
     rows = bricks * 64
     devices = n_scene * n_kd
     scene_bits = n_scene.bit_length() - 1
-    size0 = padded(2 * 7 * 256, devices)
-    size1 = padded(2 * 1024 + 7 * 128, devices)
+    sizes = [padded(n, devices) for n in (CUT, 2 * 7 * 256 - CUT, 2 * 1024, 7 * 128)]
     n_sems = 2 * scene_bits + 2 * (n_kd - 1)
     vmem = pl.BlockSpec(memory_space=pltpu.VMEM)
     smem = pl.BlockSpec(memory_space=pltpu.SMEM)
+    hbm = pl.BlockSpec(memory_space=pltpu.HBM)
 
     def reduction(size):
         return [
@@ -401,23 +443,30 @@
             pltpu.SemaphoreType.DMA((n_sems,)),
         ]
 
-    encoded, sum0, sum1 = pl.pallas_call(
+    encoded, *sums = pl.pallas_call(
         functools.partial(kernel, n_scene, n_kd, n_bits),
-        out_shape=(
-            jax.ShapeDtypeStruct((rows, 256), BF16),
-            jax.ShapeDtypeStruct((size0, 128), BF16),
-            jax.ShapeDtypeStruct((size1, 128), BF16),
-        ),
-        in_specs=[vmem, smem, smem, vmem, vmem, vmem, vmem],
-        out_specs=(vmem, vmem, vmem),
+        out_shape=[jax.ShapeDtypeStruct((rows, 256), BF16)]
+        + [jax.ShapeDtypeStruct((size, 128), BF16) for size in sizes],
+        in_specs=[hbm, smem, smem, hbm, hbm, hbm, hbm],
+        out_specs=[vmem] * 5,
         scratch_shapes=[
+            pltpu.VMEM((bricks * 512, 128), BF16),
+            pltpu.VMEM((rows, 256), BF16),
+            pltpu.VMEM((7 * 128, 128), BF16),
+            pltpu.VMEM((1024, 256), BF16),
+            pltpu.VMEM((7 * 256, 256), BF16),
+            pltpu.SemaphoreType.DMA((5,)),
             pltpu.VMEM((rows, 1024), BF16),
             pltpu.VMEM((8, rows, 7 * 128), BF16),
+            pltpu.VMEM((7 * 128, 8 * rows), BF16),
             pltpu.VMEM((rows, 1024), F32),
             pltpu.VMEM((rows, 1024), BF16),
+            pltpu.VMEM((1024, rows), BF16),
+            pltpu.VMEM((8 * rows, 128), BF16),
             pltpu.VMEM((6, rows, rows), BF16),
             pltpu.VMEM((n_bits, 2, rows, 16), BF16),
             pltpu.VMEM((n_bits * 16, rows), BF16),
+            pltpu.VMEM((rows, 7 * 256), BF16),
             pltpu.VMEM((rows, 7 * 256), BF16),
             pltpu.VMEM((n_bits, 16, 512), BF16),
             pltpu.VMEM((n_bits, 16, 512), BF16),
@@ -428,24 +477,40 @@
             pltpu.SemaphoreType.DMA((3 * n_bits,)),
             pltpu.SemaphoreType.DMA((3 * n_bits,)),
         ]
-        + reduction(size0)
-        + reduction(size1),
+        + [entry for size in sizes for entry in reduction(size)],
         compiler_params=pltpu.CompilerParams(
-            collective_id=0, has_side_effects=True, vmem_limit_bytes=48 * 2**20
+            collective_id=0, has_side_effects=True, vmem_limit_bytes=61 * 2**20
         ),
     )(
         features.reshape(bricks * 512, 128),
-        send_faces[0, 0],
-        face_source[0],
+        send_faces.reshape(1, n_bits),
+        face_source,
         cotangent.reshape(rows, 256),
         conv_one.reshape(7 * 128, 128),
         down,
         conv_two.reshape(7 * 256, 256),
     )
-    wide = 7 * 256
-    grad_two = jnp.concatenate([sum0[:wide], sum0[wide : 2 * wide]], axis=1).astype(F32)
-    grad_down = jnp.concatenate([sum1[:1024], sum1[1024:2048]], axis=1).astype(F32)
-    grad_one = sum1[2048 : 2048 + 7 * 128].astype(F32)
+    encoded, grad_one, grad_down, grad_two = pl.pallas_call(
+        finish,
+        out_shape=(
+            jax.ShapeDtypeStruct((rows, 256), BF16),
+            jax.ShapeDtypeStruct((7 * 128, 128), F32),
+            jax.ShapeDtypeStruct((1024, 256), F32),
+            jax.ShapeDtypeStruct((7 * 256, 256), F32),
+        ),
+        in_specs=[hbm] * 5,
+        out_specs=(hbm,) * 4,
+        scratch_shapes=[pltpu.VMEM((size, 128), BF16) for size in sizes]
+        + [
+            pltpu.VMEM((rows, 256), BF16),
+            pltpu.VMEM((7 * 128, 128), F32),
+            pltpu.VMEM((1024, 256), F32),
+            pltpu.VMEM((7 * 256, 256), F32),
+            pltpu.SemaphoreType.DMA((5,)),
+            pltpu.SemaphoreType.DMA((13,)),
+        ],
+        compiler_params=pltpu.CompilerParams(vmem_limit_bytes=61 * 2**20),
+    )(*sums, encoded)
     return (
         encoded.reshape(1, bricks, 64, 256),
         grad_one.reshape(7, 128, 128),

time: 68.3 us -> 62.9 us (0.921)
  local copies, waits for them, and re-layouts: 7.29 us -> 0 us
  Pallas kernels: 56.8 us -> 62 us
  other arithmetic: 3.19 us -> 0 us
    unnamed x13 -> x0, local copies, waits for them, and re-layouts: 6.44 us -> none
    pallas_call x0 -> x1, Pallas kernels: none -> 3.08 us  [on_device(): pl.pallas_call(finish, out_shape=(jax.ShapeDtypeStruct((rows, 256), BF16)...]
    convert_element_type x2 -> x0, other arithmetic: 2.39 us -> none  [the longest x1 1.35 us: on_device(): jnp.concatenate([sum0[:wide], sum0[wide:2 * wide]], axis=1).astype(F32)]
    pallas_call x1, Pallas kernels: 56.8 us -> 59 us  [on_device(): pl.pallas_call(functools.partial(kernel, n_scene, n_kd, n_bits), out_shap...]
    reshape x1 -> x0, other arithmetic: 0.8 us -> none  [on_device(): grad_one.reshape(7, 128, 128)]
    squeeze x1 -> x0, local copies, waits for them, and re-layouts: 0.74 us -> none  [on_device(): send_faces[0, 0]]
where the time goes in v2:
time: 62.9 us; the launch traced here: 62.7 us
  Pallas kernels  62 us (99%)
  between operations  0.64 us (1%)
    pallas_call x1, Pallas kernels, on_device(): pl.pallas_call(functools.partial(kernel, n_scene, n_kd, n_bits), out_shap...  59 us
    pallas_call x1, Pallas kernels, on_device(): pl.pallas_call(finish, out_shape=(jax.ShapeDtypeStruct((rows, 256), BF16)...  3.08 us

profile of v2, /device:TPU:0, one launch (start us, length us, event | category | flops | bytes accessed | tf_op | source)
XLA Modules:
  0.0 62.7 jit_solution(8101614613558804491)
XLA Ops:
  0.6 59.0 %shard_map.102 = (bf16[256,256]{1,0:T(8,128)(2,1)}, bf16[2048,128]{1,0:T(8,128)(2,1)}, bf16[1536,128]{1,0:T(8,128)(2,1)}, bf16[2048,128]{1,0:T(8,128)(2,1)}, bf16[1024,128]{1,0:T(8,128)(2,1)}) custom-call(bf16[2048,128]{1,0:T(8,128)(2,1)} %bitcast.9, s32[1,2]{1,0:T(1,128)} %bitcast.12, s32[1,4,6]{2,1,0:T(4,128)} %refs_2_.1, bf16[256,256]{1,0:T(8,128)(2,1)} %bitcast.11, ...), custom_call_target="tpu_custom_call" | custom-call | tf_op jit(solution)/shard_map/pallas_call | solution.py:446
  59.6 3.1 %shard_map.103 = (bf16[256,256]{1,0:T(8,128)(2,1)}, f32[896,128]{1,0:T(8,128)}, f32[1024,256]{1,0:T(8,128)}, f32[1792,256]{1,0:T(8,128)}) custom-call(bf16[2048,128]{1,0:T(8,128)(2,1)} %get-tuple-element.13.refs_0_, bf16[1536,128]{1,0:T(8,128)(2,1)} %get-tuple-element.14.refs_1_, bf16[2048,128]{1,0:T(8,128)(2,1)} %get-tuple-element.15.refs_2_, ...), custom_call_target="tpu_custom_call" | custom-call | tf_op jit(solution)/shard_map/pallas_call | solution.py:493

commit v3 on v2

--- a/solution.py
+++ b/solution.py
@@ -49,10 +49,10 @@
 
 
 class Reduction:
-    def __init__(self, total, staged, landed, out, sems, bits, n_scene, n_kd):
+    def __init__(self, total, staged, landed, out, sems, groups, n_scene, n_kd):
         self.total, self.staged, self.landed, self.out = total, staged, landed, out
         self.send, self.recv = sems
-        self.bits, self.n_kd = bits, n_kd
+        self.groups, self.n_kd = groups, n_kd
         self.piece = total.shape[0] // (n_scene * n_kd)
         self.scene = lax.axis_index("scene")
         self.kd = lax.axis_index("kd")
@@ -80,24 +80,28 @@
         return made
 
     def steps(self):
-        for bit in self.bits:
-            mask = 2**bit
-            mine = (self.scene // mask) % 2
-            half = self.count // 2
-            other = {"scene": self.scene + mask - 2 * mask * mine}
-            away = self.offset + (1 - mine) * half
-            keep = self.offset + mine * half
-            slot = pl.ds(self.base * self.piece, half * self.piece)
-            self.staged[slot, :] = self.total[self.rows(away, half), :].astype(BF16)
-            made = self.copy(self.staged.at[slot], self.landed.at[slot], other)
+        for group in self.groups:
+            share = self.count >> len(group)
+            digit = self.digit(group, 0)
+            keep = self.offset + digit * share
+            made = []
+            for j in range(1, 2 ** len(group)):
+                away = self.offset + self.digit(group, j) * share
+                slot = pl.ds(self.base * self.piece, share * self.piece)
+                self.staged[slot, :] = self.total[self.rows(away, share), :].astype(BF16)
+                other = {"scene": flipped(self.scene, group, j)}
+                made.append((self.copy(self.staged.at[slot], self.landed.at[slot], other), slot))
+                self.base += share
             yield
-            made.wait()
-            kept = self.rows(keep, half)
-            self.total[kept, :] = self.total[kept, :] + self.landed[slot, :].astype(F32)
-            self.base += half
-            self.count = half
+            kept = self.rows(keep, share)
+            value = self.total[kept, :]
+            for one, slot in made:
+                one.wait()
+                value = value + self.landed[slot, :].astype(F32)
+            self.total[kept, :] = value
+            self.count = share
             self.offset = keep
-            self.levels.append((other, keep, half))
+            self.levels.append((group, keep, share))
         made = []
         for j in range(1, self.n_kd):
             peer = self.peer(j)
@@ -119,20 +123,44 @@
         yield
         for one in made:
             one.wait()
-        for other, keep, half in reversed(self.levels):
-            kept = self.rows(keep, half)
-            one = self.copy(self.out.at[kept], self.out.at[kept], other)
+        for group, keep, share in reversed(self.levels):
+            kept = self.rows(keep, share)
+            made = [
+                self.copy(
+                    self.out.at[kept], self.out.at[kept], {"scene": flipped(self.scene, group, j)}
+                )
+                for j in range(1, 2 ** len(group))
+            ]
             yield
-            one.wait()
+            for one in made:
+                one.wait()
+
+    def digit(self, group, j):
+        result = 0
+        for place, bit in enumerate(group):
+            own = (self.scene // 2**bit) % 2
+            result = result + 2**place * (1 - own if j >> place & 1 else own)
+        return result
 
     def peer(self, j):
-        result = self.kd
-        bit = 1
-        while bit < self.n_kd:
-            if j & bit:
-                result = result + bit - 2 * bit * ((self.kd // bit) % 2)
-            bit *= 2
-        return result
+        return flipped(self.kd, range(self.n_kd.bit_length() - 1), j)
+
+
+def flipped(index, bits, j):
+    result = index
+    for place, bit in enumerate(bits):
+        if j >> place & 1:
+            result = result + 2**bit - 2 * 2**bit * ((index // 2**bit) % 2)
+    return result
+
+
+def groups_of(scene_bits, chain):
+    chips = list(range(1, scene_bits))
+    if chain >= 2:
+        rest = [chips[i : i + 2] for i in range(0, len(chips), 2)]
+    else:
+        rest = [[bit] for bit in (chips if chain == 0 else chips[::-1])]
+    return [[0]] + rest
 
 
 def kernel(n_scene, n_kd, n_bits, *refs):
@@ -147,7 +175,7 @@
     enc_ref, *outs = take(5)
     x_ref, cot_ref, w1_ref, dw_ref, w2_ref, in_sem = take(6)
     xp_ref, t1_ref, t1t_ref, slope_ref, patch_ref, patcht_ref, delta1_ref = take(7)
-    shift_ref, place_ref, pick_ref, t2_ref, td_ref = take(5)
+    shift_ref, place_ref, pick_ref, t2_ref, td_ref, xt_ref, arrived_ref = take(7)
     fs1, fr1, fs2, fr2, fs3, fr3, face_send, face_recv = take(8)
     bricks = source_ref.shape[1]
     rows = bricks * 64
@@ -155,13 +183,18 @@
     scene_bits = n_scene.bit_length() - 1
     kd = lax.axis_index("kd")
     scene = lax.axis_index("scene")
-    up = list(range(scene_bits))
+    greeted = set()
     chains = []
     for k in range(4):
         total, staged, landed, send, recv = take(5)
-        order = up if k % 2 == 0 else up[:1] + up[:0:-1]
+        groups = groups_of(scene_bits, k)
+        for group in groups:
+            greeted |= {
+                sum(2**bit for place, bit in enumerate(group) if j >> place & 1)
+                for j in range(1, 2 ** len(group))
+            }
         chains.append(
-            Reduction(total, staged, landed, outs[k], (send, recv), order, n_scene, n_kd)
+            Reduction(total, staged, landed, outs[k], (send, recv), groups, n_scene, n_kd)
         )
     loads = []
     for k, (src, dst) in enumerate(
@@ -175,9 +208,8 @@
     for j in range(1, n_kd):
         peer = chains[0].peer(j)
         pl.semaphore_signal(barrier, inc=1, device_id={"kd": peer}, device_id_type=MESH)
-    for bit in range(scene_bits):
-        mask = 2**bit
-        other = scene + mask - 2 * mask * ((scene // mask) % 2)
+    for j in sorted(greeted):
+        other = flipped(scene, range(scene_bits), j)
         pl.semaphore_signal(barrier, inc=1, device_id={"scene": other}, device_id_type=MESH)
 
     to = lax.broadcasted_iota(jnp.int32, (128, 128), 0)
@@ -241,29 +273,37 @@
         pieces.append(
             jnp.where(mine == 0, lanes(part, far[2 * axis]), lanes(part, far[2 * axis + 1]))
         )
-    pl.semaphore_wait(barrier, n_kd - 1 + scene_bits)
+    pl.semaphore_wait(barrier, n_kd - 1 + len(greeted))
     copies = exchange(0, fs1, fr1, pieces)
 
     row = lax.broadcasted_iota(jnp.int32, (64, rows), 0)
     col = lax.broadcasted_iota(jnp.int32, (64, rows), 1)
-    row16 = lax.broadcasted_iota(jnp.int32, (64, 16), 0)
-    col16 = lax.broadcasted_iota(jnp.int32, (64, 16), 1)
+    gap = col - row
     for s in range(6):
         axis, step = s // 2, STRIDE[s // 2]
         sign = 1 if s % 2 else -1
         border = coordinate(row, axis) == (3 if s % 2 else 0)
-        border16 = coordinate(row16, axis) == (3 if s % 2 else 0)
-        gap = col - row
-        gap16 = col16 - face_rows(row16, axis)
         for b in range(bricks):
             source = source_ref[0, b, s]
             base = jnp.where(source < local, (source // 6) * 64, -4096)
             wish = jnp.where(border, base - sign * 3 * step, b * 64 + sign * step)
             shift_ref[s, b * 64 : (b + 1) * 64, :] = one_hot(gap == wish)
-            for bit in range(axis, n_bits, 3):
-                here = jnp.where(source == local + bit, 0, -4096)
-                wish = jnp.where(border16, here, -4096)
-                place_ref[bit, s % 2, b * 64 : (b + 1) * 64, :] = one_hot(gap16 == wish)
+    row16 = lax.broadcasted_iota(jnp.int32, (64, 16), 0)
+    col16 = lax.broadcasted_iota(jnp.int32, (64, 16), 1)
+    arriving = []
+    for bit in range(n_bits):
+        axis = bit % 3
+        mine = (kd // 2**bit) % 2
+        side = 2 * axis + 1 - mine
+        arriving.append((axis, mine, side))
+        border = coordinate(row16, axis) == 3 * (1 - mine)
+        gap = col16 - face_rows(row16, axis)
+        for b in range(bricks):
+            here = jnp.where(source_ref[0, b, side] == local + bit, 0, -4096)
+            place_ref[bit, b * 64 : (b + 1) * 64, :] = one_hot(gap == jnp.where(border, here, -4096))
+
+    def tap_at(tap, width):
+        return pl.ds(pl.multiple_of(tap * width, width), width)
 
     for c in range(8):
         t1_ref[c, :, 0:128] = xp_ref[:, c * 128 : (c + 1) * 128]
@@ -276,13 +316,13 @@
             t1_ref[near, :, tap] = moved[:, k * 128 : (k + 1) * 128]
     for made in copies:
         made.wait()
-    for bit in range(n_bits):
-        for s in (2 * (bit % 3), 2 * (bit % 3) + 1):
-            tap = slice((s + 1) * 128, (s + 2) * 128)
-            moved = dot(place_ref[bit, s % 2], fr1[bit]).astype(BF16)
-            for k, c in enumerate(far[s]):
-                near = c ^ CLASS[s // 2]
-                t1_ref[near, :, tap] = t1_ref[near, :, tap] + moved[:, k * 128 : (k + 1) * 128]
+    for bit, (axis, mine, side) in enumerate(arriving):
+        tap = tap_at(side + 1, 128)
+        moved = dot(place_ref[bit], fr1[bit]).astype(BF16)
+        arrived_ref[bit] = moved
+        for k, c in enumerate(far[2 * axis + 1]):
+            near = c + CLASS[axis] * (1 - mine)
+            t1_ref[near, :, tap] = t1_ref[near, :, tap] + moved[:, k * 128 : (k + 1) * 128]
 
     load_w1.wait()
     pre_one = dot(t1_ref[...].reshape(8 * rows, 7 * 128), w1_ref[...])
@@ -301,14 +341,28 @@
     for s in range(6):
         t2_ref[:, (s + 1) * 256 : (s + 2) * 256] = dot(shift_ref[s], coarse).astype(BF16)
     for c in range(8):
-        t1t_ref[:, c * rows : (c + 1) * rows] = t1_ref[c].T
+        xt_ref[c * 128 : (c + 1) * 128, :] = xp_ref[:, c * 128 : (c + 1) * 128].T
         patcht_ref[c * 128 : (c + 1) * 128, :] = patch_ref[:, c * 128 : (c + 1) * 128].T
+        t1t_ref[0:128, c * rows : (c + 1) * rows] = xt_ref[c * 128 : (c + 1) * 128, :]
+    for s in range(6):
+        tap = slice((s + 1) * 128, (s + 2) * 128)
+        operand = jnp.concatenate([xt_ref[c * 128 : (c + 1) * 128, :] for c in far[s]], axis=0)
+        moved = dot(operand, shift_ref[s ^ 1]).astype(BF16)
+        for k, c in enumerate(far[s]):
+            near = c ^ CLASS[s // 2]
+            t1t_ref[tap, c * rows : (c + 1) * rows] = xt_ref[near * 128 : (near + 1) * 128, :]
+            t1t_ref[tap, near * rows : (near + 1) * rows] = moved[k * 128 : (k + 1) * 128]
+    for bit, (axis, mine, side) in enumerate(arriving):
+        tap = tap_at(side + 1, 128)
+        for k, c in enumerate(far[2 * axis + 1]):
+            at = tap_at(c + CLASS[axis] * (1 - mine), rows)
+            moved = arrived_ref[bit, :, k * 128 : (k + 1) * 128].T
+            t1t_ref[tap, at] = t1t_ref[tap, at] + moved
     for made in copies:
         made.wait()
-    for bit in range(n_bits):
-        for s in (2 * (bit % 3), 2 * (bit % 3) + 1):
-            tap = slice((s + 1) * 256, (s + 2) * 256)
-            t2_ref[:, tap] = t2_ref[:, tap] + dot(place_ref[bit, s % 2], fr2[bit]).astype(BF16)
+    for bit, (axis, mine, side) in enumerate(arriving):
+        tap = tap_at(side + 1, 256)
+        t2_ref[:, tap] = t2_ref[:, tap] + dot(place_ref[bit], fr2[bit]).astype(BF16)
     load_w2.wait()
     load_cot.wait()
     pre = dot(t2_ref[...], w2_ref[...])
@@ -332,11 +386,9 @@
         td_ref[:, t * 256 : (t + 1) * 256] = dot(shift_ref[s], delta).astype(BF16)
     for made in copies:
         made.wait()
-    for bit in range(n_bits):
-        for s in (2 * (bit % 3), 2 * (bit % 3) + 1):
-            t = OPPOSITE[s + 1]
-            tap = slice(t * 256, (t + 1) * 256)
-            td_ref[:, tap] = td_ref[:, tap] + dot(place_ref[bit, s % 2], fr3[bit]).astype(BF16)
+    for bit, (axis, mine, side) in enumerate(arriving):
+        tap = tap_at(2 * axis + mine + 1, 256)
+        td_ref[:, tap] = td_ref[:, tap] + dot(place_ref[bit], fr3[bit]).astype(BF16)
     pump(runs)
     back = upstream
     for t in range(7):
@@ -348,7 +400,6 @@
     fill(
         chains[2].total, jnp.concatenate([grad_down[:, 0:128], grad_down[:, 128:256]], axis=0)
     )
-    pump(runs)
     runs.append(chains[2].steps())
     pump(runs[2:])
     for c in range(8):
@@ -429,18 +480,20 @@
     devices = n_scene * n_kd
     scene_bits = n_scene.bit_length() - 1
     sizes = [padded(n, devices) for n in (CUT, 2 * 7 * 256 - CUT, 2 * 1024, 7 * 128)]
-    n_sems = 2 * scene_bits + 2 * (n_kd - 1)
+    exchanges = [
+        n_kd - 1 + sum(2 ** len(group) - 1 for group in groups_of(scene_bits, k)) for k in range(4)
+    ]
     vmem = pl.BlockSpec(memory_space=pltpu.VMEM)
     smem = pl.BlockSpec(memory_space=pltpu.SMEM)
     hbm = pl.BlockSpec(memory_space=pltpu.HBM)
 
-    def reduction(size):
+    def reduction(size, count):
         return [
             pltpu.VMEM((size, 128), F32),
             pltpu.VMEM((size, 128), BF16),
             pltpu.VMEM((size, 128), BF16),
-            pltpu.SemaphoreType.DMA((n_sems,)),
-            pltpu.SemaphoreType.DMA((n_sems,)),
+            pltpu.SemaphoreType.DMA((2 * count,)),
+            pltpu.SemaphoreType.DMA((2 * count,)),
         ]
 
     encoded, *sums = pl.pallas_call(
@@ -464,10 +517,12 @@
             pltpu.VMEM((1024, rows), BF16),
             pltpu.VMEM((8 * rows, 128), BF16),
             pltpu.VMEM((6, rows, rows), BF16),
-            pltpu.VMEM((n_bits, 2, rows, 16), BF16),
+            pltpu.VMEM((n_bits, rows, 16), BF16),
             pltpu.VMEM((n_bits * 16, rows), BF16),
             pltpu.VMEM((rows, 7 * 256), BF16),
             pltpu.VMEM((rows, 7 * 256), BF16),
+            pltpu.VMEM((1024, rows), BF16),
+            pltpu.VMEM((n_bits, rows, 512), BF16),
             pltpu.VMEM((n_bits, 16, 512), BF16),
             pltpu.VMEM((n_bits, 16, 512), BF16),
             pltpu.VMEM((n_bits, 16, 256), BF16),
@@ -477,7 +532,7 @@
             pltpu.SemaphoreType.DMA((3 * n_bits,)),
             pltpu.SemaphoreType.DMA((3 * n_bits,)),
         ]
-        + [entry for size in sizes for entry in reduction(size)],
+        + [entry for pair in zip(sizes, exchanges) for entry in reduction(*pair)],
         compiler_params=pltpu.CompilerParams(
             collective_id=0, has_side_effects=True, vmem_limit_bytes=61 * 2**20
         ),

time: 62.9 us -> 53.9 us (0.86)
  Pallas kernels: 62 us -> 53.1 us
    pallas_call x1, Pallas kernels: 59 us -> 50 us  [on_device(): pl.pallas_call(functools.partial(kernel, n_scene, n_kd, n_bits), out_shap...]
where the time goes in v3:
time: 53.9 us; the launch traced here: 53.8 us
  Pallas kernels  53.1 us (99%)
  between operations  0.64 us (1%)
    pallas_call x1, Pallas kernels, on_device(): pl.pallas_call(functools.partial(kernel, n_scene, n_kd, n_bits), out_shap...  50 us
    pallas_call x1, Pallas kernels, on_device(): pl.pallas_call(finish, out_shape=(jax.ShapeDtypeStruct((rows, 256), BF16)...  3.08 us

profile of v3, /device:TPU:0, one launch (start us, length us, event | category | flops | bytes accessed | tf_op | source)
XLA Modules:
  0.0 53.8 jit_solution(1868401666329851871)
XLA Ops:
  0.6 50.0 %shard_map.102 = (bf16[256,256]{1,0:T(8,128)(2,1)}, bf16[2048,128]{1,0:T(8,128)(2,1)}, bf16[1536,128]{1,0:T(8,128)(2,1)}, bf16[2048,128]{1,0:T(8,128)(2,1)}, bf16[1024,128]{1,0:T(8,128)(2,1)}) custom-call(bf16[2048,128]{1,0:T(8,128)(2,1)} %bitcast.9, s32[1,2]{1,0:T(1,128)} %bitcast.12, s32[1,4,6]{2,1,0:T(4,128)} %refs_2_.1, bf16[256,256]{1,0:T(8,128)(2,1)} %bitcast.11, ...), custom_call_target="tpu_custom_call" | custom-call | tf_op jit(solution)/shard_map/pallas_call | solution.py:499
  50.7 3.1 %shard_map.103 = (bf16[256,256]{1,0:T(8,128)(2,1)}, f32[896,128]{1,0:T(8,128)}, f32[1024,256]{1,0:T(8,128)}, f32[1792,256]{1,0:T(8,128)}) custom-call(bf16[2048,128]{1,0:T(8,128)(2,1)} %get-tuple-element.13.refs_0_, bf16[1536,128]{1,0:T(8,128)(2,1)} %get-tuple-element.14.refs_1_, bf16[2048,128]{1,0:T(8,128)(2,1)} %get-tuple-element.15.refs_2_, ...), custom_call_target="tpu_custom_call" | custom-call | tf_op jit(solution)/shard_map/pallas_call | solution.py:548

commit v4 on v3

--- a/solution.py
+++ b/solution.py
@@ -49,7 +49,8 @@
 
 
 class Reduction:
-    def __init__(self, total, staged, landed, out, sems, groups, n_scene, n_kd):
+    def __init__(self, total, staged, landed, out, store, sems, groups, n_scene, n_kd):
+        self.store = store
         self.total, self.staged, self.landed, self.out = total, staged, landed, out
         self.send, self.recv = sems
         self.groups, self.n_kd = groups, n_kd
@@ -134,6 +135,7 @@
             yield
             for one in made:
                 one.wait()
+        self.store.start()
 
     def digit(self, group, j):
         result = 0
@@ -154,13 +156,8 @@
     return result
 
 
-def groups_of(scene_bits, chain):
-    chips = list(range(1, scene_bits))
-    if chain >= 2:
-        rest = [chips[i : i + 2] for i in range(0, len(chips), 2)]
-    else:
-        rest = [[bit] for bit in (chips if chain == 0 else chips[::-1])]
-    return [[0]] + rest
+def groups_of(scene_bits):
+    return [[0]] + [list(range(i, min(i + 2, scene_bits))) for i in range(1, scene_bits, 2)]
 
 
 def kernel(n_scene, n_kd, n_bits, *refs):
@@ -172,8 +169,9 @@
         return taken
 
     x_hbm, send_ref, source_ref, cot_hbm, w1_hbm, dw_hbm, w2_hbm = take(7)
-    enc_ref, *outs = take(5)
+    enc_hbm, *results = take(5)
     x_ref, cot_ref, w1_ref, dw_ref, w2_ref, in_sem = take(6)
+    enc_ref, out_sem, *outs = take(6)
     xp_ref, t1_ref, t1t_ref, slope_ref, patch_ref, patcht_ref, delta1_ref = take(7)
     shift_ref, place_ref, pick_ref, t2_ref, td_ref, xt_ref, arrived_ref = take(7)
     fs1, fr1, fs2, fr2, fs3, fr3, face_send, face_recv = take(8)
@@ -187,14 +185,24 @@
     chains = []
     for k in range(4):
         total, staged, landed, send, recv = take(5)
-        groups = groups_of(scene_bits, k)
+        groups = groups_of(scene_bits)
         for group in groups:
             greeted |= {
                 sum(2**bit for place, bit in enumerate(group) if j >> place & 1)
                 for j in range(1, 2 ** len(group))
             }
         chains.append(
-            Reduction(total, staged, landed, outs[k], (send, recv), groups, n_scene, n_kd)
+            Reduction(
+                total,
+                staged,
+                landed,
+                outs[k],
+                pltpu.make_async_copy(outs[k], results[k], out_sem.at[k]),
+                (send, recv),
+                groups,
+                n_scene,
+                n_kd,
+            )
         )
     loads = []
     for k, (src, dst) in enumerate(
@@ -368,6 +376,8 @@
     pre = dot(t2_ref[...], w2_ref[...])
     g = sigmoid(pre)
     enc_ref[...] = (coarse.astype(F32) + pre * g).astype(BF16)
+    store_enc = pltpu.make_async_copy(enc_ref, enc_hbm, out_sem.at[4])
+    store_enc.start()
     upstream = cot_ref[...].astype(F32)
     delta = (upstream * (g * (1.0 + pre * (1.0 - g)))).astype(BF16)
     picked = dot(pick_ref[...], delta)
@@ -406,12 +416,15 @@
         cols = slice(c * 128, (c + 1) * 128)
         patch_grad = dot_nt(grad_coarse, dw_ref[cols, :])
         delta1_ref[c * rows : (c + 1) * rows, :] = (patch_grad * slope_ref[:, cols]).astype(BF16)
-    pump(runs)
+    pump(runs[2:])
     fill(chains[3].total, dot(t1t_ref[...], delta1_ref[...]))
     runs.append(chains[3].steps())
     pump(runs[3:])
     while runs:
         pump(runs)
+    store_enc.wait()
+    for chain in chains:
+        chain.store.wait()
 
 
 CUT = 2048
@@ -481,9 +494,8 @@
     scene_bits = n_scene.bit_length() - 1
     sizes = [padded(n, devices) for n in (CUT, 2 * 7 * 256 - CUT, 2 * 1024, 7 * 128)]
     exchanges = [
-        n_kd - 1 + sum(2 ** len(group) - 1 for group in groups_of(scene_bits, k)) for k in range(4)
+        n_kd - 1 + sum(2 ** len(group) - 1 for group in groups_of(scene_bits)) for _ in sizes
     ]
-    vmem = pl.BlockSpec(memory_space=pltpu.VMEM)
     smem = pl.BlockSpec(memory_space=pltpu.SMEM)
     hbm = pl.BlockSpec(memory_space=pltpu.HBM)
 
@@ -501,7 +513,7 @@
         out_shape=[jax.ShapeDtypeStruct((rows, 256), BF16)]
         + [jax.ShapeDtypeStruct((size, 128), BF16) for size in sizes],
         in_specs=[hbm, smem, smem, hbm, hbm, hbm, hbm],
-        out_specs=[vmem] * 5,
+        out_specs=[hbm] * 5,
         scratch_shapes=[
             pltpu.VMEM((bricks * 512, 128), BF16),
             pltpu.VMEM((rows, 256), BF16),
@@ -509,6 +521,11 @@
             pltpu.VMEM((1024, 256), BF16),
             pltpu.VMEM((7 * 256, 256), BF16),
             pltpu.SemaphoreType.DMA((5,)),
+            pltpu.VMEM((rows, 256), BF16),
+            pltpu.SemaphoreType.DMA((5,)),
+        ]
+        + [pltpu.VMEM((size, 128), BF16) for size in sizes]
+        + [
             pltpu.VMEM((rows, 1024), BF16),
             pltpu.VMEM((8, rows, 7 * 128), BF16),
             pltpu.VMEM((7 * 128, 8 * rows), BF16),

time: 53.9 us -> 54 us (level)
  no operation moved by 1% of the time
where the time goes in v4:
time: 54 us; the launch traced here: 53.8 us
  Pallas kernels  53.1 us (98%)
  between operations  0.64 us (1%)
    pallas_call x1, Pallas kernels, on_device(): pl.pallas_call(functools.partial(kernel, n_scene, n_kd, n_bits), out_shap...  50.1 us
    pallas_call x1, Pallas kernels, on_device(): pl.pallas_call(finish, out_shape=(jax.ShapeDtypeStruct((rows, 256), BF16)...  3.08 us

profile of v4, /device:TPU:0, one launch (start us, length us, event | category | flops | bytes accessed | tf_op | source)
XLA Modules:
  0.0 53.8 jit_solution(4937560761280967564)
XLA Ops:
  0.6 50.1 %shard_map.102 = (bf16[256,256]{1,0:T(8,128)(2,1)}, bf16[2048,128]{1,0:T(8,128)(2,1)}, bf16[1536,128]{1,0:T(8,128)(2,1)}, bf16[2048,128]{1,0:T(8,128)(2,1)}, bf16[1024,128]{1,0:T(8,128)(2,1)}) custom-call(bf16[2048,128]{1,0:T(8,128)(2,1)} %bitcast.9, s32[1,2]{1,0:T(1,128)} %bitcast.12, s32[1,4,6]{2,1,0:T(4,128)} %refs_2_.1, bf16[256,256]{1,0:T(8,128)(2,1)} %bitcast.11, ...), custom_call_target="tpu_custom_call" | custom-call | tf_op jit(solution)/shard_map/pallas_call | solution.py:511
  50.7 3.1 %shard_map.103 = (bf16[256,256]{1,0:T(8,128)(2,1)}, f32[896,128]{1,0:T(8,128)}, f32[1024,256]{1,0:T(8,128)}, f32[1792,256]{1,0:T(8,128)}) custom-call(bf16[2048,128]{1,0:T(8,128)(2,1)} %get-tuple-element.13.refs_0_, bf16[1536,128]{1,0:T(8,128)(2,1)} %get-tuple-element.14.refs_1_, bf16[2048,128]{1,0:T(8,128)(2,1)} %get-tuple-element.15.refs_2_, ...), custom_call_target="tpu_custom_call" | custom-call | tf_op jit(solution)/shard_map/pallas_call | solution.py:565

commit v5 on v4

--- a/solution.py
+++ b/solution.py
@@ -19,12 +19,12 @@
     return jnp.dot(a, b, preferred_element_type=F32)
 
 
-def dot_tn(a, b):
-    return lax.dot_general(a, b, (((0,), (0,)), ((), ())), preferred_element_type=F32)
-
-
 def dot_nt(a, b):
     return lax.dot_general(a, b, (((1,), (1,)), ((), ())), preferred_element_type=F32)
+
+
+def turned(identity, a):
+    return dot_nt(identity, a).astype(BF16)
 
 
 def one_hot(mask):
@@ -173,7 +173,7 @@
     x_ref, cot_ref, w1_ref, dw_ref, w2_ref, in_sem = take(6)
     enc_ref, out_sem, *outs = take(6)
     xp_ref, t1_ref, t1t_ref, slope_ref, patch_ref, patcht_ref, delta1_ref = take(7)
-    shift_ref, place_ref, pick_ref, t2_ref, td_ref, xt_ref, arrived_ref = take(7)
+    shift_ref, place_ref, pick_ref, t2_ref, td_ref, xt_ref, arrived_ref, t2t_ref = take(8)
     fs1, fr1, fs2, fr2, fs3, fr3, face_send, face_recv = take(8)
     bricks = source_ref.shape[1]
     rows = bricks * 64
@@ -229,6 +229,7 @@
         + (to // 16) % 2
     )
     arrange = one_hot(frm == wanted)
+    identity = one_hot(frm == to)
 
     face = lax.broadcasted_iota(jnp.int32, (16, rows), 0)
     voxel = lax.broadcasted_iota(jnp.int32, (16, rows), 1)
@@ -349,8 +350,12 @@
     for s in range(6):
         t2_ref[:, (s + 1) * 256 : (s + 2) * 256] = dot(shift_ref[s], coarse).astype(BF16)
     for c in range(8):
-        xt_ref[c * 128 : (c + 1) * 128, :] = xp_ref[:, c * 128 : (c + 1) * 128].T
-        patcht_ref[c * 128 : (c + 1) * 128, :] = patch_ref[:, c * 128 : (c + 1) * 128].T
+        xt_ref[c * 128 : (c + 1) * 128, :] = turned(
+            identity, xp_ref[:, c * 128 : (c + 1) * 128]
+        )
+        patcht_ref[c * 128 : (c + 1) * 128, :] = turned(
+            identity, patch_ref[:, c * 128 : (c + 1) * 128]
+        )
         t1t_ref[0:128, c * rows : (c + 1) * rows] = xt_ref[c * 128 : (c + 1) * 128, :]
     for s in range(6):
         tap = slice((s + 1) * 128, (s + 2) * 128)
@@ -364,7 +369,7 @@
         tap = tap_at(side + 1, 128)
         for k, c in enumerate(far[2 * axis + 1]):
             at = tap_at(c + CLASS[axis] * (1 - mine), rows)
-            moved = arrived_ref[bit, :, k * 128 : (k + 1) * 128].T
+            moved = turned(identity, arrived_ref[bit, :, k * 128 : (k + 1) * 128])
             t1t_ref[tap, at] = t1t_ref[tap, at] + moved
     for made in copies:
         made.wait()
@@ -383,7 +388,10 @@
     picked = dot(pick_ref[...], delta)
     copies = exchange(2, fs3, fr3, [picked[i * 16 : (i + 1) * 16] for i in range(n_bits)])
 
-    grad_two = dot_tn(t2_ref[...], delta)
+    for k in range(14):
+        at = slice(k * 128, (k + 1) * 128)
+        t2t_ref[at, :] = turned(identity, t2_ref[:, at])
+    grad_two = dot(t2t_ref[...], delta)
     flat = jnp.concatenate([grad_two[:, 0:128], grad_two[:, 128:256]], axis=0)
     fill(chains[0].total, flat[0:CUT])
     fill(chains[1].total, flat[CUT:])
@@ -540,6 +548,7 @@
             pltpu.VMEM((rows, 7 * 256), BF16),
             pltpu.VMEM((1024, rows), BF16),
             pltpu.VMEM((n_bits, rows, 512), BF16),
+            pltpu.VMEM((7 * 256, rows), BF16),
             pltpu.VMEM((n_bits, 16, 512), BF16),
             pltpu.VMEM((n_bits, 16, 512), BF16),
             pltpu.VMEM((n_bits, 16, 256), BF16),

time: 54 us -> 53.5 us (level)
  no operation moved by 1% of the time
where the time goes in v5:
time: 53.5 us; the launch traced here: 53.3 us
  Pallas kernels  52.7 us (99%)
  between operations  0.64 us (1%)
    pallas_call x1, Pallas kernels, on_device(): pl.pallas_call(functools.partial(kernel, n_scene, n_kd, n_bits), out_shap...  49.6 us
    pallas_call x1, Pallas kernels, on_device(): pl.pallas_call(finish, out_shape=(jax.ShapeDtypeStruct((rows, 256), BF16)...  3.08 us

profile of v5, /device:TPU:0, one launch (start us, length us, event | category | flops | bytes accessed | tf_op | source)
XLA Modules:
  0.0 53.3 jit_solution(12517737071886846338)
XLA Ops:
  0.6 49.6 %shard_map.102 = (bf16[256,256]{1,0:T(8,128)(2,1)}, bf16[2048,128]{1,0:T(8,128)(2,1)}, bf16[1536,128]{1,0:T(8,128)(2,1)}, bf16[2048,128]{1,0:T(8,128)(2,1)}, bf16[1024,128]{1,0:T(8,128)(2,1)}) custom-call(bf16[2048,128]{1,0:T(8,128)(2,1)} %bitcast.9, s32[1,2]{1,0:T(1,128)} %bitcast.12, s32[1,4,6]{2,1,0:T(4,128)} %refs_2_.1, bf16[256,256]{1,0:T(8,128)(2,1)} %bitcast.11, ...), custom_call_target="tpu_custom_call" | custom-call | tf_op jit(solution)/shard_map/pallas_call | solution.py:519
  50.2 3.1 %shard_map.103 = (bf16[256,256]{1,0:T(8,128)(2,1)}, f32[896,128]{1,0:T(8,128)}, f32[1024,256]{1,0:T(8,128)}, f32[1792,256]{1,0:T(8,128)}) custom-call(bf16[2048,128]{1,0:T(8,128)(2,1)} %get-tuple-element.13.refs_0_, bf16[1536,128]{1,0:T(8,128)(2,1)} %get-tuple-element.14.refs_1_, bf16[2048,128]{1,0:T(8,128)(2,1)} %get-tuple-element.15.refs_2_, ...), custom_call_target="tpu_custom_call" | custom-call | tf_op jit(solution)/shard_map/pallas_call | solution.py:574

commit v6 on v5

--- a/solution.py
+++ b/solution.py
@@ -156,8 +156,13 @@
     return result
 
 
-def groups_of(scene_bits):
-    return [[0]] + [list(range(i, min(i + 2, scene_bits))) for i in range(1, scene_bits, 2)]
+def groups_of(scene_bits, chain):
+    chips = list(range(1, scene_bits))
+    if chain >= 2:
+        rest = [chips[i : i + 2] for i in range(0, len(chips), 2)]
+    else:
+        rest = [[bit] for bit in (chips if chain == 0 else chips[::-1])]
+    return [[0]] + rest
 
 
 def kernel(n_scene, n_kd, n_bits, *refs):
@@ -185,7 +190,7 @@
     chains = []
     for k in range(4):
         total, staged, landed, send, recv = take(5)
-        groups = groups_of(scene_bits)
+        groups = groups_of(scene_bits, k)
         for group in groups:
             greeted |= {
                 sum(2**bit for place, bit in enumerate(group) if j >> place & 1)
@@ -424,7 +429,7 @@
         cols = slice(c * 128, (c + 1) * 128)
         patch_grad = dot_nt(grad_coarse, dw_ref[cols, :])
         delta1_ref[c * rows : (c + 1) * rows, :] = (patch_grad * slope_ref[:, cols]).astype(BF16)
-    pump(runs[2:])
+    pump(runs)
     fill(chains[3].total, dot(t1t_ref[...], delta1_ref[...]))
     runs.append(chains[3].steps())
     pump(runs[3:])
@@ -502,7 +507,7 @@
     scene_bits = n_scene.bit_length() - 1
     sizes = [padded(n, devices) for n in (CUT, 2 * 7 * 256 - CUT, 2 * 1024, 7 * 128)]
     exchanges = [
-        n_kd - 1 + sum(2 ** len(group) - 1 for group in groups_of(scene_bits)) for _ in sizes
+        n_kd - 1 + sum(2 ** len(group) - 1 for group in groups_of(scene_bits, k)) for k in range(4)
     ]
     smem = pl.BlockSpec(memory_space=pltpu.SMEM)
     hbm = pl.BlockSpec(memory_space=pltpu.HBM)

time: 53.5 us -> 54.2 us (1.013)
  Pallas kernels: 52.7 us -> 53.4 us
    pallas_call x1, Pallas kernels: 49.6 us -> 50.3 us  [on_device(): pl.pallas_call(functools.partial(kernel, n_scene, n_kd, n_bits), out_shap...]
where the time goes in v6:
time: 54.2 us; the launch traced here: 54 us
  Pallas kernels  53.4 us (99%)
  between operations  0.64 us (1%)
    pallas_call x1, Pallas kernels, on_device(): pl.pallas_call(functools.partial(kernel, n_scene, n_kd, n_bits), out_shap...  50.3 us
    pallas_call x1, Pallas kernels, on_device(): pl.pallas_call(finish, out_shape=(jax.ShapeDtypeStruct((rows, 256), BF16)...  3.08 us

profile of v6, /device:TPU:0, one launch (start us, length us, event | category | flops | bytes accessed | tf_op | source)
XLA Modules:
  0.0 54.0 jit_solution(12591649268329358683)
XLA Ops:
  0.6 50.3 %shard_map.102 = (bf16[256,256]{1,0:T(8,128)(2,1)}, bf16[2048,128]{1,0:T(8,128)(2,1)}, bf16[1536,128]{1,0:T(8,128)(2,1)}, bf16[2048,128]{1,0:T(8,128)(2,1)}, bf16[1024,128]{1,0:T(8,128)(2,1)}) custom-call(bf16[2048,128]{1,0:T(8,128)(2,1)} %bitcast.9, s32[1,2]{1,0:T(1,128)} %bitcast.12, s32[1,4,6]{2,1,0:T(4,128)} %refs_2_.1, bf16[256,256]{1,0:T(8,128)(2,1)} %bitcast.11, ...), custom_call_target="tpu_custom_call" | custom-call | tf_op jit(solution)/shard_map/pallas_call | solution.py:524
  50.9 3.1 %shard_map.103 = (bf16[256,256]{1,0:T(8,128)(2,1)}, f32[896,128]{1,0:T(8,128)}, f32[1024,256]{1,0:T(8,128)}, f32[1792,256]{1,0:T(8,128)}) custom-call(bf16[2048,128]{1,0:T(8,128)(2,1)} %get-tuple-element.13.refs_0_, bf16[1536,128]{1,0:T(8,128)(2,1)} %get-tuple-element.14.refs_1_, bf16[2048,128]{1,0:T(8,128)(2,1)} %get-tuple-element.15.refs_2_, ...), custom_call_target="tpu_custom_call" | custom-call | tf_op jit(solution)/shard_map/pallas_call | solution.py:579
